TPU v7x, 128 devices: a whole 4x4x4 slice. The times are simulated.
128 devices in a mesh: dp: 32 (over y, z_lo, x), grad: 4 (over z_hi, core).
Axes of the slice: x: 4, y: 4, z: 4 (z_hi: 2, z_lo: 2; z = z_hi * 2 + z_lo), core: 2. Of those that a mesh axis runs over, the one named last changes fastest.
Arguments:
- grads: float32 [64, 4, 256, 1024], P(None, 'grad', 'dp'), may hold values from -6 to 6
- basis_slots: bfloat16 [32, 4, 2, 1024, 1024], P('dp', 'grad'), may hold values from -0.1875 to 0.1875
- owners: int32 [64, 2], P('dp'), may hold values from 0 to 3, as said below
- eig_in: float32 [64, 1024], P('dp'), may hold values from 0.1 to 3
- eig_out: float32 [64, 1024], P('dp'), may hold values from 0.1 to 3
Outputs:
- precond: float32 [64, 4, 256, 1024], P(None, 'grad', 'dp')
Inputs may be any that keep to these rules, and one draw needn't show every extreme that they name: `owners`: each entry is a grad index; within each group of 2 consecutive modules no grad index owns more than 2 of the group's 2 * 2 bases, and at least one grad index owns exactly 2.
All inputs are finite; a program needn't handle non-finite values.
Results may differ from a plain program's by a relative error of at most 0.0003.
Values may be sent and summed in bfloat16 or wider, within the bound.
No kernel may reach another device: no remote copies, remote signals or barrier semaphores. Data moves between devices by JAX's collectives and lax.ppermute only.
A program may use at most 128 MiB of HBM per device.

v0:
```python
import jax
import jax.numpy as jnp
from jax import lax
from jax.sharding import PartitionSpec as P


def broadcast(value, axis, source):
    kept = jnp.where(lax.axis_index(axis) == source, value, 0).astype(value.dtype)
    return lax.psum(kept, axis)


def local(grads, basis_slots, owners, eig_in, eig_out):
    high = lax.Precision.HIGHEST
    local_count = eig_in.shape[0]
    my_group = lax.axis_index("grad")
    gathered = lax.all_to_all(grads, "dp", split_axis=0, concat_axis=2, tiled=True)
    row_count = gathered.shape[2]
    row_start = my_group * row_count
    flat = owners.reshape(-1)
    order = jnp.arange(flat.shape[0], dtype=jnp.int32)
    same = flat[:, None] == flat[None, :]
    earlier = order[None, :] < order[:, None]
    slot_table = jnp.sum((same & earlier).astype(jnp.int32), axis=1)
    own_slots = basis_slots[0, 0]
    results = []
    for module in range(local_count):
        owner_a = flat[2 * module]
        owner_g = flat[2 * module + 1]
        own_a = lax.dynamic_index_in_dim(own_slots, slot_table[2 * module], 0, keepdims=False)
        own_g = lax.dynamic_index_in_dim(own_slots, slot_table[2 * module + 1], 0, keepdims=False)
        basis_a = broadcast(own_a, "grad", owner_a).astype(jnp.float32)
        basis_g = broadcast(own_g, "grad", owner_g).astype(jnp.float32)
        grad_rows = gathered[module, 0]
        basis_g_rows = lax.dynamic_slice_in_dim(basis_g, row_start, row_count, 0)
        rotated_rows = jnp.dot(grad_rows, basis_a, precision=high)
        basis_g_cols = lax.dynamic_slice_in_dim(basis_g, row_start, row_count, 1)
        eigen_rows = lax.dot_general(
            basis_g_cols,
            lax.all_gather(rotated_rows, "grad", axis=0, tiled=True),
            (((0,), (0,)), ((), ())),
            precision=high,
        )
        eig_g_rows = lax.dynamic_slice_in_dim(eig_out[module], row_start, row_count, 0)
        scaled_rows = eigen_rows / (eig_g_rows[:, None] * eig_in[module][None, :] + 0.1)
        back_rows = lax.dot_general(scaled_rows, basis_a, (((1,), (1,)), ((), ())), precision=high)
        final_rows = jnp.dot(
            basis_g_rows, lax.all_gather(back_rows, "grad", axis=0, tiled=True), precision=high
        )
        results.append(final_rows)
    stacked = jnp.stack(results, axis=0)[:, None]
    return lax.all_to_all(stacked, "dp", split_axis=2, concat_axis=0, tiled=True)


def solution(mesh):
    return jax.shard_map(
        local,
        mesh=mesh,
        in_specs=(
            P(None, "grad", "dp", None),
            P("dp", "grad", None, None, None),
            P("dp", None),
            P("dp", None),
            P("dp", None),
        ),
        out_specs=P(None, "grad", "dp", None),
        check_vma=False,
    )
```

profile of v0, /device:TPU:0, one launch (start us, length us, event | category | flops | bytes accessed | tf_op | source)
XLA Modules:
  0.0 423.9 jit_solution(10114299557421550797)
XLA Ops:
  6.5 0.0 all-reduce.3.cloned.1.call-start
  6.5 0.8 reshape.35
  7.3 0.2 convert_reduce_fusion
  7.5 0.6 fusion.12
  13.2 0.7 fusion.11
  18.9 7.0 %select_bitcast_fusion.3 = (bf16[1024,1024]{1,0:T(8,128)(2,1)}, bf16[1024,1024]{1,0:T(8,128)(2,1)}, bf16[1024,1024]{1,0:T(8,128)(2,1)}, bf16[1024,1024]{1,0:T(8,128)(2,1)}) fusion(bf16[1,1,2,1024,1024]{4,3,2,1,0:T(8,128)(2,1)} %param.6, s32[]{:T(128)S(6)} %select_n.60, pred[]{:T(512)S(6)} %eq.25, s32[]{:T(128)S(6)} %select_n.65, pred[]{:T(512)S(6)} %eq.29, ...), kind=kLoop, calls=%fused_computation.4 | loop fusion | flops 4194304 | bytes 16777236 | tf_op jit(solution)/shard_map/jit(_where)/select_n | solution.py:8
  25.9 0.0 copy-start.2
  25.9 0.0 all-reduce.3.cloned.1.call-update
  25.9 0.0 all-gather.5.cloned.1.call-start
  26.0 1.5 copy-done.2
  27.5 36.5 %all_to_all.33 = f32[64,1,8,1024]{3,2,1,0:T(8,128)} all-to-all(f32[64,1,8,1024]{3,2,1,0:T(8,128)S(1)} %copy-done.2), channel_id=1, replica_groups=mesh['dp'=32,'grad'=4] {'dp'}, dimensions={0} | all-to-all | bytes 4194304 | tf_op jit(solution)/shard_map/all_to_all | solution.py:16
  64.0 147.9 %all-reduce.3.cloned.1.call-done = (bf16[1024,1024]{1,0:T(8,128)(2,1)}, bf16[1024,1024]{1,0:T(8,128)(2,1)}, bf16[1024,1024]{1,0:T(8,128)(2,1)}, bf16[1024,1024]{1,0:T(8,128)(2,1)}) async-done(((bf16[1024,1024]{1,0:T(8,128)(2,1)}, bf16[1024,1024]{1,0:T(8,128)(2,1)}, bf16[1024,1024]{1,0:T(8,128)(2,1)}, bf16[1024,1024]{1,0:T(8,128)(2,1)}), (bf16[1024,1024]{1,0:T(8,128)(2,1)}, bf16[1024,1024]{1,0:T(8,128)(2,1)}, ...) | async-done | bytes 8388624 | tf_op jit(solution)/shard_map/psum | solution.py:9
  211.9 0.0 copy-start
  211.9 5.3 %convolution_bitcast_fusion.3 = f32[256,1024]{0,1:T(8,128)} fusion(bf16[1024,1024]{1,0:T(8,128)(2,1)} %get-tuple-element.7, f32[2,1,32,8,1024]{4,3,0,2,1:T(8,128)} %bitcast.54), kind=kOutput, calls=%fused_computation.10 | convolution fusion | flops 3221225472 | bytes 4194304 | tf_op jit(solution)/shard_map/dot_general | solution.py:35
  217.3 0.0 all-gather.5.cloned.1.call-update
  217.3 0.0 all-gather.9.cloned.1.call-start
  217.4 0.0 copy-done
  217.4 0.0 copy-start.3
  217.4 0.0 copy-start.4
  217.4 4.6 %convolution_bitcast_fusion.1 = f32[256,1024]{0,1:T(8,128)} fusion(bf16[1024,1024]{1,0:T(8,128)(2,1)S(1)} %copy-done, f32[2,1,32,8,1024]{4,3,0,2,1:T(8,128)} %bitcast.55), kind=kOutput, calls=%fused_computation.7 | convolution fusion | flops 3221225472 | bytes 4194304 | tf_op jit(solution)/shard_map/dot_general | solution.py:35
  222.0 0.0 all-gather.9.cloned.1.call-update
  222.0 0.0 all-gather.7.cloned.1.call-start
  222.1 0.0 copy-done.3
  222.1 0.0 copy-done.4
  222.1 33.2 %all-gather.5.cloned.1.call-done = f32[1024,1024]{0,1:T(8,128)} async-done(((f32[256,1024]{0,1:T(8,128)}), f32[1024,1024]{0,1:T(8,128)}) %all-gather.5.cloned.1.call-update) | async-done | bytes 4194320 | tf_op jit(solution)/shard_map/all_gather | solution.py:39
  255.3 0.0 copy-start.1
  255.3 5.0 %convolution_divide_fusion.1 = f32[256,1024]{1,0:T(8,128)S(1)} fusion(f32[1024,1024]{0,1:T(8,128)} %all-gather.5.cloned.1.call-done, f32[1024]{0:T(1024)S(1)} %bitcast.57, f32[256]{0:T(256)S(1)} %bitcast.58, bf16[1024,1024]{1,0:T(8,128)(2,1)} %get-tuple-element.8, s32[]{:T(128)S(6)} %select_n.63), kind=kOutput, calls=%fused_computation.9 | convolution fusion | flops 3222011904 | bytes 5772292 | tf_op jit(solution)/shard_map/dot_general | solution.py:37
  260.4 0.0 copy-done.1
  260.4 2.9 fusion.13
  263.3 0.0 all-gather.7.cloned.1.call-update
  263.3 0.2 all-gather.11.cloned.1.call-start
  263.5 31.4 %all-gather.9.cloned.1.call-done = f32[1024,1024]{0,1:T(8,128)} async-done(((f32[256,1024]{0,1:T(8,128)}), f32[1024,1024]{0,1:T(8,128)}) %all-gather.9.cloned.1.call-update) | async-done | bytes 4194320 | tf_op jit(solution)/shard_map/all_gather | solution.py:39
  294.9 4.9 %convolution_divide_fusion = f32[256,1024]{1,0:T(8,128)S(1)} fusion(f32[1024,1024]{0,1:T(8,128)} %all-gather.9.cloned.1.call-done, f32[1024]{0:T(1024)S(1)} %bitcast.56, f32[256]{0:T(256)S(1)} %bitcast.59, bf16[1024,1024]{1,0:T(8,128)(2,1)} %get-tuple-element.6, s32[]{:T(128)S(6)} %select_n.63), kind=kOutput, calls=%fused_computation.6 | convolution fusion | flops 3222011904 | bytes 5772292 | tf_op jit(solution)/shard_map/dot_general | solution.py:37
  299.8 2.8 fusion.14
  302.6 0.0 all-gather.11.cloned.1.call-update
  302.6 31.7 %all-gather.7.cloned.1.call-done = f32[1024,1024]{1,0:T(8,128)} async-done(((f32[256,1024]{1,0:T(8,128)}), f32[1024,1024]{1,0:T(8,128)}) %all-gather.7.cloned.1.call-update) | async-done | bytes 4194320 | tf_op jit(solution)/shard_map/all_gather | solution.py:47
  334.3 4.5 %convolution_bitcast_fusion.2 = f32[1,256,1024]{2,1,0:T(8,128)S(1)} fusion(f32[1024,1024]{1,0:T(8,128)} %all-gather.7.cloned.1.call-done, bf16[1024,1024]{1,0:T(8,128)(2,1)} %get-tuple-element.8, s32[]{:T(128)S(6)} %select_n.63), kind=kOutput, calls=%fused_computation.8 | convolution fusion | flops 3221225472 | bytes 5767172 | tf_op jit(solution)/shard_map/dot_general | solution.py:46
  338.9 34.9 %all-gather.11.cloned.1.call-done = f32[1024,1024]{1,0:T(8,128)} async-done(((f32[256,1024]{1,0:T(8,128)}), f32[1024,1024]{1,0:T(8,128)}) %all-gather.11.cloned.1.call-update) | async-done | bytes 4194320 | tf_op jit(solution)/shard_map/all_gather | solution.py:47
  373.8 4.5 %convolution_bitcast_fusion = f32[1,256,1024]{2,1,0:T(8,128)S(1)} fusion(f32[1024,1024]{1,0:T(8,128)} %all-gather.11.cloned.1.call-done, bf16[1024,1024]{1,0:T(8,128)(2,1)} %get-tuple-element.6, s32[]{:T(128)S(6)} %select_n.63), kind=kOutput, calls=%fused_computation.5 | convolution fusion | flops 3221225472 | bytes 5767172 | tf_op jit(solution)/shard_map/dot_general | solution.py:46
  378.3 0.2 maximum_bitcast_fusion
  378.5 1.6 copy.9
  380.1 35.1 %all_to_all.34 = f32[2,1,256,1024]{3,0,1,2:T(2,128)S(1)} all-to-all(f32[2,1,256,1024]{3,0,1,2:T(2,128)S(1)} %copy.9), channel_id=1, replica_groups=mesh['dp'=32,'grad'=4] {'dp'}, dimensions={2} | all-to-all | bytes 4194304 | tf_op jit(solution)/shard_map/all_to_all | solution.py:51
  415.2 2.2 copy.10
  (4 shorter events, 0.0 us)
Async XLA Ops:
  6.5 205.4 %all-reduce.3.cloned.1.call-start = ((), (), s32[]{:S(2)}) async-start(), calls=%async_computation.6 | async-start | bytes 16777216 | tf_op jit(solution)/shard_map/psum | solution.py:9
  25.9 1.6 copy-start.2
  25.9 229.4 %all-gather.5.cloned.1.call-start = ((), (), s32[]{:S(2)}) async-start(), calls=%async_computation.2 | async-start | bytes 5242880 | tf_op jit(solution)/shard_map/all_gather | solution.py:39
  211.9 5.4 %copy-start = (bf16[1024,1024]{1,0:T(8,128)(2,1)S(1)}, bf16[1024,1024]{1,0:T(8,128)(2,1)}, u32[]{:S(2)}) copy-start(bf16[1024,1024]{1,0:T(8,128)(2,1)} %get-tuple-element.5) | copy-start | bytes 6291460
  217.3 77.6 %all-gather.9.cloned.1.call-start = ((), (), s32[]{:S(2)}) async-start(), calls=%async_computation.4 | async-start | bytes 5242880 | tf_op jit(solution)/shard_map/all_gather | solution.py:39
  217.4 4.7 %copy-start.3 = (f32[2,1024]{1,0:T(2,128)S(1)}, f32[2,1024]{1,0:T(2,128)}, u32[]{:S(2)}) copy-start(f32[2,1024]{1,0:T(2,128)} %param.9) | copy-start | bytes 24580
  217.4 4.7 %copy-start.4 = (f32[2,1024]{1,0:T(2,128)S(1)}, f32[2,1024]{1,0:T(2,128)}, u32[]{:S(2)}) copy-start(f32[2,1024]{1,0:T(2,128)} %param.8) | copy-start | bytes 24580
  222.0 112.3 %all-gather.7.cloned.1.call-start = ((), (), s32[]{:S(2)}) async-start(), calls=%async_computation.3 | async-start | bytes 5242880 | tf_op jit(solution)/shard_map/all_gather | solution.py:47
  255.3 5.0 %copy-start.1 = (bf16[1024,1024]{1,0:T(8,128)(2,1)S(1)}, bf16[1024,1024]{1,0:T(8,128)(2,1)}, u32[]{:S(2)}) copy-start(bf16[1024,1024]{1,0:T(8,128)(2,1)} %get-tuple-element.7) | copy-start | bytes 6291460
  263.3 110.5 %all-gather.11.cloned.1.call-start = ((), (), s32[]{:S(2)}) async-start(), calls=%async_computation.5 | async-start | bytes 5242880 | tf_op jit(solution)/shard_map/all_gather | solution.py:47
Sparse Core Ops, SparseCore 0:
  26.0 185.8 all-reduce.2
  217.4 37.8 all-gather.4
  257.0 37.8 all-gather.8
  296.4 37.8 all-gather.6
  335.9 37.8 all-gather.10
where the time goes:
time: 425 us; the launch traced here: 424 us
  waiting for transfers between devices  279 us (66%)
  blocking collectives  71.6 us (17%)
  matrix products  34.6 us (8%)
  between operations  23.4 us (6%)
  local copies, waits for them, and re-layouts  7.44 us (2%)
  other arithmetic  7.35 us (2%)
    psum x1, waiting for transfers between devices, broadcast(): return lax.psum(kept, axis)  148 us
    all_gather x2, waiting for transfers between devices, local(): lax.all_gather(back_rows, 'grad', axis=0, tiled=True)  66.6 us
    all_gather x2, waiting for transfers between devices, local(): lax.all_gather(rotated_rows, 'grad', axis=0, tiled=True)  64.6 us
    all_to_all x1, blocking collectives, local(): lax.all_to_all(grads, 'dp', split_axis=0, concat_axis=2, tiled=True)  36.5 us
    all_to_all x1, blocking collectives, local(): lax.all_to_all(stacked, 'dp', split_axis=2, concat_axis=0, tiled=True)  35.1 us
    dot_general x2, matrix products, local(): rotated_rows = jnp.dot(grad_rows, basis_a, precision=high)  9.92 us
    dot_general x2, matrix products, local(): lax.dot_general(basis_g_cols, lax.all_gather(rotated_rows, 'grad', axis=0...  9.91 us
    dot_general x2, matrix products, local(): jnp.dot(basis_g_rows, lax.all_gather(back_rows, 'grad', axis=0, tiled=Tru...  9.08 us
  transfers between devices with their start and end apart: 5, of which 5 were waited for; matrix products, arithmetic and copies ran while one was open for 6% of the time, Pallas kernels for 0%

commit v1 on v0

v1 whole, which is shorter than its diff:
```python
import functools

import jax
import jax.numpy as jnp
from jax import lax
from jax.experimental import pallas as pl
from jax.experimental.pallas import tpu as pltpu
from jax.sharding import Mesh, PartitionSpec as P

D = 1024
HALF = 512
WIDE = D + 128
VMEM_LIMIT = 50 * 1024 * 1024
F32 = jnp.float32
BF16 = jnp.bfloat16
I16 = jnp.int16
ANY = pl.BlockSpec(memory_space=pl.ANY)
VMEM = pl.BlockSpec(memory_space=pltpu.VMEM)
SMEM = pl.BlockSpec(memory_space=pltpu.SMEM)
CORE_SWAP = [(0, 1), (1, 0)]


def params(**kw):
    return pltpu.CompilerParams(vmem_limit_bytes=VMEM_LIMIT, **kw)


def basis_of(owners, module, side):
    flat = [owners[0, 0], owners[0, 1], owners[1, 0], owners[1, 1]]
    slot = []
    for k in range(4):
        total = jnp.int32(0)
        for j in range(k):
            total = total + (flat[j] == flat[k]).astype(jnp.int32)
        slot.append(total)
    first = module == 0
    owner = jnp.where(first, flat[side], flat[2 + side])
    return owner, jnp.where(first, slot[side], slot[2 + side])


def split(x):
    high = x.astype(BF16)
    return high, (x - high.astype(F32)).astype(BF16)


def quantize(x):
    most = jnp.maximum(jnp.max(jnp.abs(x), axis=1, keepdims=True), 1e-25)
    step = most * (1.0 / 32700.0)
    exponent = jnp.floor(jnp.log2(step))
    mantissa = jnp.clip(jnp.ceil(step * jnp.exp2(14.0 - exponent)), 1.0, 32767.0)
    scale = mantissa * jnp.exp2(exponent - 14.0)
    whole = jnp.clip(jnp.round(x * (1.0 / scale)), -32767.0, 32767.0)
    lane = lax.broadcasted_iota(jnp.int32, (x.shape[0], 128), 1)
    tail = jnp.where(lane < 64, exponent, mantissa)
    return whole.astype(jnp.int32).astype(I16), tail.astype(jnp.int32).astype(I16)


def scale_of(tail):
    tail = tail.astype(jnp.int32).astype(F32)
    return tail[:, 64:65] * jnp.exp2(tail[:, 0:1] - 14.0)


def quantize_kernel(x_ref, out_ref):
    whole, tail = quantize(x_ref[...])
    out_ref[:, :D] = whole
    out_ref[:, D:] = tail


def quantize_rows(x):
    rows = x.shape[0]
    return pl.pallas_call(
        quantize_kernel,
        grid=(4,),
        in_specs=[pl.BlockSpec((rows // 4, D), lambda i: (i, 0))],
        out_specs=pl.BlockSpec((rows // 4, WIDE), lambda i: (i, 0)),
        out_shape=jax.ShapeDtypeStruct((rows, WIDE), I16),
        compiler_params=params(),
        cost_estimate=pl.CostEstimate(flops=0, bytes_accessed=rows * D * 6, transcendentals=0),
        name="quantize",
    )(x)


def restore_kernel(x_ref, out_ref):
    out_ref[...] = x_ref[:, :D].astype(jnp.int32).astype(F32) * scale_of(x_ref[:, D:])


def restore_rows(x):
    rows = x.shape[0]
    return pl.pallas_call(
        restore_kernel,
        grid=(4,),
        in_specs=[pl.BlockSpec((rows // 4, WIDE), lambda i: (i, 0))],
        out_specs=pl.BlockSpec((rows // 4, D), lambda i: (i, 0)),
        out_shape=jax.ShapeDtypeStruct((rows, D), F32),
        compiler_params=params(),
        cost_estimate=pl.CostEstimate(flops=0, bytes_accessed=rows * D * 6, transcendentals=0),
        name="restore",
    )(x)


def pick_kernel(owners, slots, other, out_a, out_g, sem):
    chip, core = lax.axis_index("zh"), lax.axis_index("core")
    mine, beside = 2 * chip + core, 2 * chip + 1 - core
    start = pl.multiple_of(core * HALF, HALF)
    for side, out in ((0, out_a), (1, out_g)):
        owner, slot = basis_of(owners, 1 - chip, side)
        for holder, source in ((mine, slots), (beside, other)):

            @pl.when(owner == holder)
            def _():
                if side == 0:
                    part = source.at[slot, pl.ds(start, HALF), :]
                else:
                    part = source.at[slot, :, pl.ds(start, HALF)]
                copy = pltpu.make_async_copy(part, out, sem)
                copy.start()
                copy.wait()


def pick(owners, slots, other):
    return pl.pallas_call(
        pick_kernel,
        in_specs=[SMEM, ANY, ANY],
        out_specs=[ANY, ANY],
        out_shape=[jax.ShapeDtypeStruct((HALF, D), BF16), jax.ShapeDtypeStruct((D, HALF), BF16)],
        scratch_shapes=[pltpu.SemaphoreType.DMA],
        compiler_params=params(),
        name="pick",
    )(owners, slots, other)


def load_rows(owners, slots, other, half, half_beside, out, sem):
    chip, core = lax.axis_index("zh"), lax.axis_index("core")
    mine, beside = 2 * chip + core, 2 * chip + 1 - core
    owner, slot = basis_of(owners, chip, 0)
    for holder, source in ((mine, slots), (beside, other)):

        @pl.when(owner == holder)
        def _():
            copy = pltpu.make_async_copy(source.at[slot], out, sem)
            copy.start()
            copy.wait()

    @pl.when((owner != mine) & (owner != beside))
    def _():
        for part, at in ((half, core), (half_beside, 1 - core)):
            copy = pltpu.make_async_copy(part, out.at[pl.ds(pl.multiple_of(at * HALF, HALF), HALF), :], sem)
            copy.start()
            copy.wait()


def load_columns(owners, slots, other, half, which, out, sem):
    chip, core = lax.axis_index("zh"), lax.axis_index("core")
    mine, beside = 2 * chip + core, 2 * chip + 1 - core
    owner, slot = basis_of(owners, chip, 1)
    start = pl.multiple_of(which * HALF, HALF)
    for holder, source in ((mine, slots), (beside, other)):

        @pl.when(owner == holder)
        def _():
            copy = pltpu.make_async_copy(source.at[slot, :, pl.ds(start, HALF)], out, sem)
            copy.start()
            copy.wait()

    @pl.when((owner != mine) & (owner != beside))
    def _():
        copy = pltpu.make_async_copy(half, out, sem)
        copy.start()
        copy.wait()


def rotate_kernel(owners, rows, rows_beside, slots, other, half, half_beside, high_ref, low_ref, basis, sem):
    core = lax.axis_index("core")
    load_rows(owners, slots, other, half, half_beside, basis, sem)
    for source, at in ((rows, core), (rows_beside, 1 - core)):
        for chip in range(2):
            block = source[...].astype(jnp.int32).astype(F32).reshape(32, 2, 8, WIDE)[:, chip].reshape(256, WIDE)
            scale = block[:, D + 64 : D + 65] * jnp.exp2(block[:, D : D + 1] - 14.0)
            high, low = split(block[:, :D])
            start = pl.multiple_of((2 * chip + at) * 256, 256)
            for col in range(0, D, 256):
                part = basis[:, col : col + 256]
                got = jnp.dot(high, part, preferred_element_type=F32) + jnp.dot(low, part, preferred_element_type=F32)
                got_high, got_low = split((got * scale).T)
                high_ref[col : col + 256, pl.ds(start, 256)] = got_high
                low_ref[col : col + 256, pl.ds(start, 256)] = got_low


def rotate(owners, rows, rows_beside, slots, other, half, half_beside):
    return pl.pallas_call(
        rotate_kernel,
        in_specs=[SMEM, VMEM, VMEM, ANY, ANY, ANY, ANY],
        out_specs=[VMEM, VMEM],
        out_shape=[jax.ShapeDtypeStruct((D, D), BF16)] * 2,
        scratch_shapes=[pltpu.VMEM((D, D), BF16), pltpu.SemaphoreType.DMA],
        compiler_params=params(),
        cost_estimate=pl.CostEstimate(flops=4 * D**3, bytes_accessed=9 * D * D, transcendentals=0),
        name="rotate",
    )(owners, rows, rows_beside, slots, other, half, half_beside)


def eigen_part(which, qg, high_ref, low_ref, eig_in, eig_out, add):
    chip, core = lax.axis_index("zh"), lax.axis_index("core")
    first = pl.multiple_of(core * 256, 256)
    eig_g = eig_out[pl.ds(chip, 1), pl.ds(pl.multiple_of(which * HALF, HALF), HALF)]
    tops = [qg[pl.ds(first, 256), :], qg[pl.ds(first + HALF, 256), :]]
    for row in range(0, D, 256):
        eigen = jnp.dot(high_ref[row : row + 256, :], qg[...], preferred_element_type=F32)
        eigen = eigen + jnp.dot(low_ref[row : row + 256, :], qg[...], preferred_element_type=F32)
        eig_a = jnp.broadcast_to(eig_in[pl.ds(chip, 1), row : row + 256], (128, 256)).T[:, 0:1]
        high, low = split(eigen / (eig_a * eig_g + 0.1))
        for at in range(2):
            got = lax.dot_general(tops[at], high, (((1,), (1,)), ((), ())), preferred_element_type=F32)
            got = got + lax.dot_general(tops[at], low, (((1,), (1,)), ((), ())), preferred_element_type=F32)
            add(at * 256, row, got)


def first_kernel(owners, high_ref, low_ref, eig_in, eig_out, slots, other, half, out_ref, qg, sem):
    core = lax.axis_index("core")
    load_columns(owners, slots, other, half, core, qg, sem)

    def add(row, col, got):
        out_ref[row : row + 256, col : col + 256] = got

    eigen_part(core, qg, high_ref, low_ref, eig_in, eig_out, add)


def first_half(owners, high, low, eig_in, eig_out, slots, other, half):
    return pl.pallas_call(
        first_kernel,
        in_specs=[SMEM, VMEM, VMEM, VMEM, VMEM, ANY, ANY, ANY],
        out_specs=VMEM,
        out_shape=jax.ShapeDtypeStruct((HALF, D), F32),
        scratch_shapes=[pltpu.VMEM((D, HALF), BF16), pltpu.SemaphoreType.DMA],
        compiler_params=params(),
        cost_estimate=pl.CostEstimate(flops=3 * D**3, bytes_accessed=7 * D * D, transcendentals=0),
        name="first_half",
    )(owners, high, low, eig_in, eig_out, slots, other, half)


def second_kernel(owners, high_ref, low_ref, eig_in, eig_out, slots, other, half, so_far, half_a, half_a_beside,
                  out_ref, qg, qa, back, sem):
    core = lax.axis_index("core")
    load_columns(owners, slots, other, half, 1 - core, qg, sem)
    load_rows(owners, slots, other, half_a, half_a_beside, qa, sem)

    def add(row, col, got):
        back[row : row + 256, col : col + 256] = so_far[row : row + 256, col : col + 256] + got

    eigen_part(1 - core, qg, high_ref, low_ref, eig_in, eig_out, add)
    for row in range(0, 256, 128):
        pieces = []
        for at in range(2):
            high, low = split(back[at * 256 + row : at * 256 + row + 128, :])
            got = lax.dot_general(high, qa[...], (((1,), (1,)), ((), ())), preferred_element_type=F32)
            got = got + lax.dot_general(low, qa[...], (((1,), (1,)), ((), ())), preferred_element_type=F32)
            pieces.append(got.reshape(16, 1, 8, D))
        whole, tail = quantize(jnp.concatenate(pieces, axis=1).reshape(256, D))
        out_ref[2 * row : 2 * row + 256, :D] = whole
        out_ref[2 * row : 2 * row + 256, D:] = tail


def second_half(owners, high, low, eig_in, eig_out, slots, other, half, so_far, half_a, half_a_beside):
    return pl.pallas_call(
        second_kernel,
        in_specs=[SMEM, VMEM, VMEM, VMEM, VMEM, ANY, ANY, ANY, VMEM, ANY, ANY],
        out_specs=VMEM,
        out_shape=jax.ShapeDtypeStruct((HALF, WIDE), I16),
        scratch_shapes=[
            pltpu.VMEM((D, HALF), BF16),
            pltpu.VMEM((D, D), BF16),
            pltpu.VMEM((HALF, D), F32),
            pltpu.SemaphoreType.DMA,
        ],
        compiler_params=params(),
        cost_estimate=pl.CostEstimate(flops=5 * D**3, bytes_accessed=10 * D * D, transcendentals=0),
        name="second_half",
    )(owners, high, low, eig_in, eig_out, slots, other, half, so_far, half_a, half_a_beside)


def local(grads, basis_slots, owners, eig_in, eig_out):
    def across(x):
        return lax.ppermute(x, "zh", CORE_SWAP)

    def beside(x):
        return lax.ppermute(x, "core", CORE_SWAP)

    def everywhere(x):
        x = x.reshape(64, 8, WIDE)
        return lax.all_to_all(x, ("dp", "zh"), split_axis=0, concat_axis=0, tiled=True).reshape(HALF, WIDE)

    slots = basis_slots[0, 0]
    other = beside(slots)
    packed = quantize_rows(grads.reshape(HALF, D))
    send_a, send_g = pick(owners, slots, other)
    half_a = across(send_a)
    rows = everywhere(packed)
    half_g = across(send_g)
    rows_beside = beside(rows)
    half_a_beside = beside(half_a)
    high, low = rotate(owners, rows, rows_beside, slots, other, half_a, half_a_beside)
    half_g_beside = beside(half_g)
    so_far = first_half(owners, high, low, eig_in, eig_out, slots, other, half_g)
    out = second_half(
        owners, high, low, eig_in, eig_out, slots, other, half_g_beside, so_far, half_a, half_a_beside
    )
    return restore_rows(everywhere(out)).reshape(64, 1, 8, D)


def solution(mesh):
    fine = Mesh(mesh.devices.reshape(32, 2, 2), ("dp", "zh", "core"))
    grad = ("zh", "core")
    return jax.shard_map(
        local,
        mesh=fine,
        in_specs=(
            P(None, grad, "dp", None),
            P("dp", grad, None, None, None),
            P("dp", None),
            P("dp", None),
            P("dp", None),
        ),
        out_specs=P(None, grad, "dp", None),
        check_vma=False,
    )
```

time: 425 us -> 199 us (0.47)
  waiting for transfers between devices: 279 us -> 45.9 us
  Pallas kernels: 0 us -> 104 us
  blocking collectives: 71.6 us -> 29.4 us
  matrix products: 34.6 us -> 0 us
  between operations: 23.4 us -> 0.12 us
  starting transfers between devices: 0.35 us -> 15.1 us
  other arithmetic: 7.35 us -> 0 us
    psum x1 -> x0, waiting for transfers between devices: 148 us -> none  [broadcast(): return lax.psum(kept, axis)]
    all_gather x4 -> x0, waiting for transfers between devices: 131 us -> none  [the longest x2 66.6 us: local(): lax.all_gather(back_rows, 'grad', axis=0, tiled=True)]
    pallas_call x0 -> x6, Pallas kernels: none -> 104 us  [the longest x1 66.3 us: pick(): pl.pallas_call(pick_kernel, in_specs=[SMEM, ANY, ANY], out_specs=[ANY, AN...]
    ppermute x0 -> x6, waiting for transfers between devices: none -> 45.9 us  [the longest x2 45.9 us: across(): return lax.ppermute(x, 'zh', CORE_SWAP)]
    all_to_all x2 -> x1, blocking collectives: 71.6 us -> 29.4 us  [everywhere(): lax.all_to_all(x, ('dp', 'zh'), split_axis=0, concat_axis=0, tiled=True)]
    dot_general x8 -> x0, matrix products: 34.6 us -> none  [the longest x2 9.92 us: local(): rotated_rows = jnp.dot(grad_rows, basis_a, precision=high)]
    all_to_all x0 -> x1, starting transfers between devices: none -> 11.5 us  [everywhere(): lax.all_to_all(x, ('dp', 'zh'), split_axis=0, concat_axis=0, tiled=True)]
    select_n x1 -> x0, other arithmetic: 6.98 us -> none  [broadcast(): jnp.where(lax.axis_index(axis) == source, value, 0).astype(value.dtype)]
  transfers between devices with their start and end apart: 5 -> 7, of which waited for: 5 -> 2; matrix products, arithmetic and copies ran while one was open for 6% -> 0% of each run, Pallas kernels for 0% -> 43%
where the time goes in v1:
time: 199 us
  Pallas kernels  104 us (52%)
  waiting for transfers between devices  45.9 us (23%)
  blocking collectives  29.4 us (15%)
  starting transfers between devices  15.1 us (8%)
  local copies, waits for them, and re-layouts  3.94 us (2%)
    pallas_call x1, Pallas kernels, pick(): pl.pallas_call(pick_kernel, in_specs=[SMEM, ANY, ANY], out_specs=[ANY, AN...  66.3 us
    ppermute x2, waiting for transfers between devices, across(): return lax.ppermute(x, 'zh', CORE_SWAP)  45.9 us
    all_to_all x1, blocking collectives, everywhere(): lax.all_to_all(x, ('dp', 'zh'), split_axis=0, concat_axis=0, tiled=True)  29.4 us
    pallas_call x1, Pallas kernels, second_half(): pl.pallas_call(second_kernel, in_specs=[SMEM, VMEM, VMEM, VMEM, VMEM, ANY...  16.3 us
    all_to_all x1, starting transfers between devices, everywhere(): lax.all_to_all(x, ('dp', 'zh'), split_axis=0, concat_axis=0, tiled=True)  11.5 us
    pallas_call x1, Pallas kernels, rotate(): pl.pallas_call(rotate_kernel, in_specs=[SMEM, VMEM, VMEM, ANY, ANY, ANY,...  9.73 us
    pallas_call x1, Pallas kernels, first_half(): pl.pallas_call(first_kernel, in_specs=[SMEM, VMEM, VMEM, VMEM, VMEM, ANY,...  7.48 us
  transfers between devices with their start and end apart: 7, of which 2 were waited for; matrix products, arithmetic and copies ran while one was open for 0% of the time, Pallas kernels for 43%

profile of v1, /device:TPU:0, one launch (start us, length us, event | category | flops | bytes accessed | tf_op | source)
XLA Modules:
  0.0 198.6 jit_solution(15348247744767867131)
XLA Ops:
  0.0 0.0 collective-permute-start.1
  0.0 0.0 copy-start.1
  0.0 1.6 copy-done.1
  1.6 0.0 copy-start.4
  1.6 2.0 %quantize.1 = s16[512,1152]{1,0:T(8,128)(2,1)} custom-call(f32[512,1024]{1,0:T(8,128)S(1)} %bitcast.10), custom_call_target="tpu_custom_call" | custom-call | bytes 3145728 | tf_op jit(solution)/shard_map/quantize/pallas_call | solution.py:70
  3.6 11.5 %all-to-all-start = ((s16[64,8,1152]{2,1,0:T(8,128)(2,1)}), s16[64,8,1152]{2,1,0:T(8,128)(2,1)S(1)}, u32[]{:S(2)}, u32[]{:S(2)}) async-start(s16[64,8,1152]{2,1,0:T(8,128)(2,1)} %bitcast.1), calls=%async_computation | async-start | bytes 2359296 | tf_op jit(solution)/shard_map/all_to_all | solution.py:289
  15.1 0.0 collective-permute-done.1.other
  15.2 0.0 copy-done.4
  15.2 66.3 %pick.1 = (bf16[512,1024]{1,0:T(8,128)(2,1)}, bf16[1024,512]{1,0:T(8,128)(2,1)}) custom-call(s32[2,2]{1,0:T(2,128)S(1)} %copy-done.4, bf16[2,1024,1024]{2,1,0:T(8,128)(2,1)} %bitcast.14, bf16[2,1024,1024]{2,1,0:T(8,128)(2,1)} %collective-permute-done.1.other), custom_call_target="tpu_custom_call" | custom-call | tf_op jit(solution)/shard_map/pick/pallas_call | solution.py:120
  81.5 0.1 collective-permute-start.2
  81.6 3.5 %collective-permute-start.4 = (bf16[1024,512]{1,0:T(8,128)(2,1)}, bf16[1024,512]{1,0:T(8,128)(2,1)S(1)}, u32[]{:S(2)}, u32[]{:S(2)}) collective-permute-start(bf16[1024,512]{1,0:T(8,128)(2,1)} %get-tuple-element.12), channel_id=1, source_target_pairs={{0,2},{2,0},{1,3},{3,1},{4,6},{6,4},{5,7},{7,5},{8,10},{10,8},{9,1... | collective-permute-start | bytes 3145736 | tf_op jit(solution)/shard_map/ppermute | solution.py:282
  85.1 0.0 all-to-all-done
  85.1 0.0 copy-start.2
  85.1 0.0 copy-start.3
  85.1 0.0 collective-permute-start
  85.1 24.2 %collective-permute-done.2.half.half_a = bf16[512,1024]{1,0:T(8,128)(2,1)S(1)} collective-permute-done((bf16[512,1024]{1,0:T(8,128)(2,1)}, bf16[512,1024]{1,0:T(8,128)(2,1)S(1)}, u32[]{:S(2)}, u32[]{:S(2)}) %collective-permute-start.2) | collective-permute-done | bytes 1048608 | tf_op jit(solution)/shard_map/ppermute | solution.py:282
  109.3 0.0 collective-permute-start.3
  109.3 21.8 %collective-permute-done.4.half = bf16[1024,512]{1,0:T(8,128)(2,1)S(1)} collective-permute-done((bf16[1024,512]{1,0:T(8,128)(2,1)}, bf16[1024,512]{1,0:T(8,128)(2,1)S(1)}, u32[]{:S(2)}, u32[]{:S(2)}) %collective-permute-start.4) | collective-permute-done | bytes 1048608 | tf_op jit(solution)/shard_map/ppermute | solution.py:282
  131.0 0.0 collective-permute-start.5
  131.0 0.0 collective-permute-done.rows_beside
  131.0 0.0 copy-start.5
  131.0 0.0 collective-permute-done.3.half_beside.half_a_beside
  131.1 1.0 copy-done.5
  132.1 9.7 %rotate.1 = (bf16[1024,1024]{1,0:T(8,128)(2,1)}, bf16[1024,1024]{1,0:T(8,128)(2,1)}) custom-call(s32[2,2]{1,0:T(2,128)S(1)} %copy-done.4, s16[512,1152]{1,0:T(8,128)(2,1)S(1)} %bitcast.12, s16[512,1152]{1,0:T(8,128)(2,1)} %copy-done.5, bf16[2,1024,1024]{2,1,0:T(8,128)(2,1)} %bitcast.15, bf16[2,1024,1024]{2,1,0:T(8,128)(2,1)} %collective-permute-done.1.other, ...), custom_call_target="tpu_custom_call" | custom-call | flops 4294967296 | bytes 9437184 | tf_op jit(solution)/shard_map/rotate/pallas_call | solution.py:189
  141.8 0.0 copy-done.2
  141.8 0.0 copy-done.3
  141.8 7.5 %first_half.1.so_far = f32[512,1024]{1,0:T(8,128)S(1)} custom-call(s32[2,2]{1,0:T(2,128)S(1)} %copy-done.4, bf16[1024,1024]{1,0:T(8,128)(2,1)} %get-tuple-element.10.high_ref, bf16[1024,1024]{1,0:T(8,128)(2,1)} %get-tuple-element.11.low_ref, f32[2,1024]{1,0:T(2,128)S(1)} %copy-done.2, f32[2,1024]{1,0:T(2,128)S(1)} %copy-done.3, ...), custom_call_target="tpu_custom_call" | custom-call | flops 3221225472 | bytes 7340032 | tf_op jit(solution)/shard_map/first_half/pallas_call | solution.py:228
  149.3 0.0 copy-start
  149.3 1.3 copy-done
  150.6 0.0 collective-permute-done.5.half
  150.6 16.3 %second_half.1 = s16[512,1152]{1,0:T(8,128)(2,1)} custom-call(s32[2,2]{1,0:T(2,128)S(1)} %copy-done.4, bf16[1024,1024]{1,0:T(8,128)(2,1)} %get-tuple-element.10.high_ref, bf16[1024,1024]{1,0:T(8,128)(2,1)} %get-tuple-element.11.low_ref, f32[2,1024]{1,0:T(2,128)S(1)} %copy-done.2, f32[2,1024]{1,0:T(2,128)S(1)} %copy-done.3, bf16[2,1024,1024]{2,1,0:T(8,128)(2,1)} %bitcast.17, ...), custom_call_target="tpu_custom_call" | custom-call | flops 5368709120 | bytes 10485760 | tf_op jit(solution)/shard_map/second_half/pallas_call | solution.py:263
  167.0 29.4 %all_to_all.10 = s16[64,8,1152]{2,1,0:T(8,128)(2,1)S(1)} all-to-all(s16[64,8,1152]{2,1,0:T(8,128)(2,1)} %bitcast.18), channel_id=1, replica_groups=mesh['dp'=32,'zh'=2,'core'=2] {'dp','zh'}, dimensions={0} | all-to-all | bytes 2359296 | tf_op jit(solution)/shard_map/all_to_all | solution.py:289
  196.4 2.1 %restore.1 = f32[512,1024]{1,0:T(8,128)} custom-call(s16[512,1152]{1,0:T(8,128)(2,1)S(1)} %bitcast.9), custom_call_target="tpu_custom_call" | custom-call | bytes 3145728 | tf_op jit(solution)/shard_map/restore/pallas_call | solution.py:88
Async XLA Ops:
  0.0 15.1 %collective-permute-start.1 = (bf16[2,1024,1024]{2,1,0:T(8,128)(2,1)}, bf16[2,1024,1024]{2,1,0:T(8,128)(2,1)}, u32[]{:S(2)}, u32[]{:S(2)}) collective-permute-start(bf16[2,1024,1024]{2,1,0:T(8,128)(2,1)} %bitcast.13), channel_id=1, source_target_pairs={{0,1},{1,0},{2,3},{3,2},{4,5},{5,4},{6,7},{7,6},{8,9},{9,8},{10,11... | collective-permute-start | bytes 12582920 | tf_op jit(solution)/shard_map/ppermute | solution.py:285
  0.0 1.6 copy-start.1
  1.6 13.6 %copy-start.4 = (s32[2,2]{1,0:T(2,128)S(1)}, s32[2,2]{1,0:T(2,128)}, u32[]{:S(2)}) copy-start(s32[2,2]{1,0:T(2,128)} %owners.7) | copy-start | bytes 52
  3.6 81.4 %all-to-all-start = ((s16[64,8,1152]{2,1,0:T(8,128)(2,1)}), s16[64,8,1152]{2,1,0:T(8,128)(2,1)S(1)}, u32[]{:S(2)}, u32[]{:S(2)}) async-start(s16[64,8,1152]{2,1,0:T(8,128)(2,1)} %bitcast.1), calls=%async_computation | async-start | bytes 2359296 | tf_op jit(solution)/shard_map/all_to_all | solution.py:289
  81.5 27.8 %collective-permute-start.2 = (bf16[512,1024]{1,0:T(8,128)(2,1)}, bf16[512,1024]{1,0:T(8,128)(2,1)S(1)}, u32[]{:S(2)}, u32[]{:S(2)}) collective-permute-start(bf16[512,1024]{1,0:T(8,128)(2,1)} %get-tuple-element.9), channel_id=1, source_target_pairs={{0,2},{2,0},{1,3},{3,1},{4,6},{6,4},{5,7},{7,5},{8,10},{10,8},{9,1... | collective-permute-start | bytes 3145736 | tf_op jit(solution)/shard_map/ppermute | solution.py:282
  81.6 49.5 %collective-permute-start.4 = (bf16[1024,512]{1,0:T(8,128)(2,1)}, bf16[1024,512]{1,0:T(8,128)(2,1)S(1)}, u32[]{:S(2)}, u32[]{:S(2)}) collective-permute-start(bf16[1024,512]{1,0:T(8,128)(2,1)} %get-tuple-element.12), channel_id=1, source_target_pairs={{0,2},{2,0},{1,3},{3,1},{4,6},{6,4},{5,7},{7,5},{8,10},{10,8},{9,1... | collective-permute-start | bytes 3145736 | tf_op jit(solution)/shard_map/ppermute | solution.py:282
  85.1 56.7 %copy-start.2 = (f32[2,1024]{1,0:T(2,128)S(1)}, f32[2,1024]{1,0:T(2,128)}, u32[]{:S(2)}) copy-start(f32[2,1024]{1,0:T(2,128)} %eig_in.3) | copy-start | bytes 24580
  85.1 56.7 %copy-start.3 = (f32[2,1024]{1,0:T(2,128)S(1)}, f32[2,1024]{1,0:T(2,128)}, u32[]{:S(2)}) copy-start(f32[2,1024]{1,0:T(2,128)} %eig_out.3) | copy-start | bytes 24580
  85.1 45.9 %collective-permute-start = (s16[512,1152]{1,0:T(8,128)(2,1)S(1)}, s16[512,1152]{1,0:T(8,128)(2,1)S(1)}, u32[]{:S(2)}, u32[]{:S(2)}) collective-permute-start(s16[512,1152]{1,0:T(8,128)(2,1)S(1)} %bitcast.11), channel_id=1, source_target_pairs={{0,1},{1,0},{2,3},{3,2},{4,5},{5,4},{6,7},{7,6},{8,9},{9,8},{10,11... | collective-permute-start | bytes 3538952 | tf_op jit(solution)/shard_map/ppermute | solution.py:285
  109.3 21.8 %collective-permute-start.3 = (bf16[512,1024]{1,0:T(8,128)(2,1)S(1)}, bf16[512,1024]{1,0:T(8,128)(2,1)S(1)}, u32[]{:S(2)}, u32[]{:S(2)}) collective-permute-start(bf16[512,1024]{1,0:T(8,128)(2,1)S(1)} %collective-permute-done.2.half.half_a), channel_id=1, source_target_pairs={{0,1},{1,0},{2,3},{3,2},{4,5},{5,4},{6,7},{7,6},{8,9},{9,8},{10,11... | collective-permute-start | bytes 3145736 | tf_op jit(solution)/shard_map/ppermute | solution.py:285
  131.0 19.6 %collective-permute-start.5 = (bf16[1024,512]{1,0:T(8,128)(2,1)S(1)}, bf16[1024,512]{1,0:T(8,128)(2,1)S(1)}, u32[]{:S(2)}, u32[]{:S(2)}) collective-permute-start(bf16[1024,512]{1,0:T(8,128)(2,1)S(1)} %collective-permute-done.4.half), channel_id=1, source_target_pairs={{0,1},{1,0},{2,3},{3,2},{4,5},{5,4},{6,7},{7,6},{8,9},{9,8},{10,11... | collective-permute-start | bytes 3145736 | tf_op jit(solution)/shard_map/ppermute | solution.py:285
  131.0 1.0 copy-start.5
  149.3 1.3 copy-start

commit v2 on v1

v2 whole, which is shorter than its diff:
```python
import jax
import jax.numpy as jnp
from jax import lax
from jax.experimental import pallas as pl
from jax.experimental.pallas import tpu as pltpu
from jax.sharding import Mesh, PartitionSpec as P

D = 1024
HALF = 512
QUARTER = 256
LEAD = HALF + QUARTER
WIDE = D + 128
F32 = jnp.float32
BF16 = jnp.bfloat16
I16 = jnp.int16
ANY = pl.BlockSpec(memory_space=pl.ANY)
HBM = pl.BlockSpec(memory_space=pltpu.HBM)
VMEM = pl.BlockSpec(memory_space=pltpu.VMEM)
SMEM = pl.BlockSpec(memory_space=pltpu.SMEM)
CORE_SWAP = [(0, 1), (1, 0)]


def params(mebibytes):
    return pltpu.CompilerParams(vmem_limit_bytes=mebibytes * 1024 * 1024)


def basis_of(owners, module, side):
    flat = [owners[0, 0], owners[0, 1], owners[1, 0], owners[1, 1]]
    slot = []
    for k in range(4):
        total = jnp.int32(0)
        for j in range(k):
            total = total + (flat[j] == flat[k]).astype(jnp.int32)
        slot.append(total)
    first = module == 0
    owner = jnp.where(first, flat[side], flat[2 + side])
    return owner, jnp.where(first, slot[side], slot[2 + side])


def split(x):
    high = x.astype(BF16)
    return high, (x - high.astype(F32)).astype(BF16)


def quantize(x):
    most = jnp.maximum(jnp.max(jnp.abs(x), axis=1, keepdims=True), 1e-25)
    step = most * (1.0 / 32700.0)
    exponent = jnp.floor(jnp.log2(step))
    mantissa = jnp.clip(jnp.ceil(step * jnp.exp2(14.0 - exponent)), 1.0, 32767.0)
    scale = mantissa * jnp.exp2(exponent - 14.0)
    whole = jnp.clip(jnp.round(x * (1.0 / scale)), -32767.0, 32767.0)
    lane = lax.broadcasted_iota(jnp.int32, (x.shape[0], 128), 1)
    tail = jnp.where(lane < 64, exponent, mantissa)
    return whole.astype(jnp.int32).astype(I16), tail.astype(jnp.int32).astype(I16)


def scale_of(tail):
    tail = tail.astype(jnp.int32).astype(F32)
    return tail[:, 64:65] * jnp.exp2(tail[:, 0:1] - 14.0)


def quantize_kernel(x_ref, out_ref):
    whole, tail = quantize(x_ref[...])
    out_ref[:, :D] = whole
    out_ref[:, D:] = tail


def quantize_rows(x):
    rows = x.shape[0]
    return pl.pallas_call(
        quantize_kernel,
        grid=(4,),
        in_specs=[pl.BlockSpec((rows // 4, D), lambda i: (i, 0))],
        out_specs=pl.BlockSpec((rows // 4, WIDE), lambda i: (i, 0)),
        out_shape=jax.ShapeDtypeStruct((rows, WIDE), I16),
        compiler_params=params(12),
        cost_estimate=pl.CostEstimate(flops=0, bytes_accessed=rows * D * 6, transcendentals=0),
        name="quantize",
    )(x)


def restore_kernel(x_ref, out_ref):
    out_ref[...] = x_ref[:, :D].astype(jnp.int32).astype(F32) * scale_of(x_ref[:, D:])


def restore_rows(x):
    rows = x.shape[0]
    return pl.pallas_call(
        restore_kernel,
        grid=(4,),
        in_specs=[pl.BlockSpec((rows // 4, WIDE), lambda i: (i, 0))],
        out_specs=pl.BlockSpec((rows // 4, D), lambda i: (i, 0)),
        out_shape=jax.ShapeDtypeStruct((rows, D), F32),
        compiler_params=params(12),
        cost_estimate=pl.CostEstimate(flops=0, bytes_accessed=rows * D * 6, transcendentals=0),
        name="restore",
    )(x)


def place(owners, module, side, chip, core):
    owner, slot = basis_of(owners, module, side)
    return owner == 2 * chip + core, owner == 2 * chip + 1 - core, slot


def columns(ref, start, size):
    return ref.at[:, pl.ds(pl.multiple_of(start, size), size)]


def run_copies(items, sem):
    for act in ("start", "wait"):
        for at, (wanted, source, out) in enumerate(items):

            @pl.when(wanted)
            def _():
                getattr(pltpu.make_async_copy(source, out, sem.at[at]), act)()


def give_kernel(owners, slots, out, sem):
    chip, core = lax.axis_index("zh"), lax.axis_index("core")
    has_a, _, slot_a = place(owners, 1 - chip, 0, chip, core)
    has_g, _, slot_g = place(owners, 1 - chip, 1, chip, core)
    items = [
        (has_a, columns(slots.at[slot_a], (1 - core) * HALF, HALF), out.at[:, :HALF]),
        (has_g, columns(slots.at[slot_g], (1 - core) * QUARTER, QUARTER), out.at[:, HALF:]),
    ]
    run_copies(items, sem)


def give(owners, slots):
    return pl.pallas_call(
        give_kernel,
        in_specs=[SMEM, HBM],
        out_specs=VMEM,
        out_shape=jax.ShapeDtypeStruct((D, LEAD), BF16),
        scratch_shapes=[pltpu.SemaphoreType.DMA((2,))],
        compiler_params=params(8),
        cost_estimate=pl.CostEstimate(flops=0, bytes_accessed=3 * D * D, transcendentals=0),
        name="give",
    )(owners, slots)


def pick_kernel(owners, slots, given, out, sem):
    chip, core = lax.axis_index("zh"), lax.axis_index("core")
    has_a, beside_a, slot_a = place(owners, 1 - chip, 0, chip, core)
    has_g, beside_g, slot_g = place(owners, 1 - chip, 1, chip, core)
    items = [
        (has_a, columns(slots.at[slot_a], core * HALF, HALF), out.at[:, :HALF]),
        (beside_a, given.at[:, :HALF], out.at[:, :HALF]),
        (has_g, columns(slots.at[slot_g], core * QUARTER, QUARTER), out.at[:, HALF:]),
        (beside_g, given.at[:, HALF:], out.at[:, HALF:]),
    ]
    run_copies(items, sem)


def pick(owners, slots, given):
    return pl.pallas_call(
        pick_kernel,
        in_specs=[SMEM, HBM, ANY],
        out_specs=VMEM,
        out_shape=jax.ShapeDtypeStruct((D, LEAD), BF16),
        scratch_shapes=[pltpu.SemaphoreType.DMA((4,))],
        compiler_params=params(8),
        cost_estimate=pl.CostEstimate(flops=0, bytes_accessed=3 * D * D, transcendentals=0),
        name="pick",
    )(owners, slots, given)


def hold_kernel(owners, slots, other, out, out_a, out_g, sem):
    chip, core = lax.axis_index("zh"), lax.axis_index("core")
    has, beside, slot = place(owners, 1 - chip, 1, chip, core)
    items = [(has, columns(slots.at[slot], HALF + core * QUARTER, QUARTER), out)]
    items.append((beside, columns(other.at[slot], HALF + core * QUARTER, QUARTER), out))
    for side, kept in enumerate((out_a, out_g)):
        has, beside, slot = place(owners, chip, side, chip, core)
        items += [(has, slots.at[slot], kept), (beside, other.at[slot], kept)]
    run_copies(items, sem)


def hold(owners, slots, other):
    return pl.pallas_call(
        hold_kernel,
        in_specs=[SMEM, HBM, HBM],
        out_specs=[VMEM] * 3,
        out_shape=[jax.ShapeDtypeStruct((D, QUARTER), BF16)] + [jax.ShapeDtypeStruct((D, D), BF16)] * 2,
        scratch_shapes=[pltpu.SemaphoreType.DMA((6,))],
        compiler_params=params(10),
        cost_estimate=pl.CostEstimate(flops=0, bytes_accessed=12 * D * D, transcendentals=0),
        name="hold",
    )(owners, slots, other)


def gather(owners, side, kept, kept_at, part, part_beside, part_at, size, out):
    chip, core = lax.axis_index("zh"), lax.axis_index("core")
    has, beside, _ = place(owners, chip, side, chip, core)

    @pl.when(has | beside)
    def _():
        out[...] = kept[:, kept_at : kept_at + 2 * size]

    @pl.when(jnp.logical_not(has | beside))
    def _():
        for source, at in ((part, core), (part_beside, 1 - core)):
            out[:, pl.ds(pl.multiple_of(at * size, size), size)] = source[:, part_at : part_at + size]


def rotate(rows, rows_beside, basis, high_ref, low_ref):
    core = lax.axis_index("core")
    for source, at in ((rows, core), (rows_beside, 1 - core)):
        for chip in range(2):
            block = source[...].astype(jnp.int32).astype(F32).reshape(32, 2, 8, WIDE)[:, chip].reshape(256, WIDE)
            scale = block[:, D + 64 : D + 65] * jnp.exp2(block[:, D : D + 1] - 14.0)
            high, low = split(block[:, :D])
            both = jnp.concatenate([high, low], axis=0)
            start = pl.multiple_of((2 * chip + at) * 256, 256)
            got = jnp.dot(both, basis[...], preferred_element_type=F32)
            got_high, got_low = split(((got[:256] + got[256:]) * scale).T)
            high_ref[:, pl.ds(start, 256)] = got_high
            low_ref[:, pl.ds(start, 256)] = got_low


def eigen_part(which, qg, high_ref, low_ref, eig_in, eig_out, add):
    chip, core = lax.axis_index("zh"), lax.axis_index("core")
    first = pl.multiple_of(core * 256, 256)
    eig_g = eig_out[pl.ds(chip, 1), which * HALF : (which + 1) * HALF]
    tops = jnp.concatenate([qg[pl.ds(first, 256), :], qg[pl.ds(first + HALF, 256), :]], axis=0)
    for row in range(0, D, 512):
        both = jnp.concatenate([high_ref[row : row + 512, :], low_ref[row : row + 512, :]], axis=0)
        eigen = jnp.dot(both, qg[...], preferred_element_type=F32)
        eigen = eigen[:512] + eigen[512:]
        eig_a = jnp.broadcast_to(eig_in[pl.ds(chip, 1), row : row + 512], (128, 512)).T[:, 0:1]
        high, low = split(eigen / (eig_a * eig_g + 0.1))
        got = lax.dot_general(tops, high, (((1,), (1,)), ((), ())), preferred_element_type=F32)
        got = got + lax.dot_general(tops, low, (((1,), (1,)), ((), ())), preferred_element_type=F32)
        add(0, row, got)


def begin_kernel(owners, rows, rows_beside, kept_a, kept_g, lead, lead_beside, eig_in, eig_out,
                 high_ref, low_ref, qa, out_ref, qg):
    gather(owners, 0, kept_a, 0, lead, lead_beside, 0, HALF, qa)
    gather(owners, 1, kept_g, 0, lead, lead_beside, HALF, QUARTER, qg)
    rotate(rows, rows_beside, qa, high_ref, low_ref)

    def add(row, col, got):
        out_ref[:, col : col + 512] = got

    eigen_part(0, qg, high_ref, low_ref, eig_in, eig_out, add)


def begin(owners, rows, rows_beside, kept_a, kept_g, lead, lead_beside, eig_in, eig_out):
    return pl.pallas_call(
        begin_kernel,
        in_specs=[SMEM] + [VMEM] * 8,
        out_specs=[VMEM] * 4,
        out_shape=[jax.ShapeDtypeStruct((D, D), BF16)] * 3 + [jax.ShapeDtypeStruct((HALF, D), F32)],
        scratch_shapes=[pltpu.VMEM((D, HALF), BF16)],
        compiler_params=params(24),
        cost_estimate=pl.CostEstimate(flops=7 * D**3, bytes_accessed=20 * D * D, transcendentals=0),
        name="begin",
    )(owners, rows, rows_beside, kept_a, kept_g, lead, lead_beside, eig_in, eig_out)


def finish_kernel(owners, high_ref, low_ref, qa, so_far, kept_g, rest, rest_beside, eig_in, eig_out,
                  out_ref, qg, back, final):
    gather(owners, 1, kept_g, HALF, rest, rest_beside, 0, QUARTER, qg)

    def add(row, col, got):
        back[:, col : col + 512] = so_far[:, col : col + 512] + got

    eigen_part(1, qg, high_ref, low_ref, eig_in, eig_out, add)
    high, low = split(back[...])
    both = jnp.concatenate([high, low], axis=0)
    for col in range(0, D, 512):
        got = lax.dot_general(both, qa[col : col + 512, :], (((1,), (1,)), ((), ())), preferred_element_type=F32)
        final[:, col : col + 512] = got[:HALF] + got[HALF:]
    for row in range(0, 256, 128):
        pieces = [final[at * 256 + row : at * 256 + row + 128, :].reshape(16, 1, 8, D) for at in range(2)]
        whole, tail = quantize(jnp.concatenate(pieces, axis=1).reshape(256, D))
        out_ref[2 * row : 2 * row + 256, :D] = whole
        out_ref[2 * row : 2 * row + 256, D:] = tail


def finish(owners, high, low, qa, so_far, kept_g, rest, rest_beside, eig_in, eig_out):
    return pl.pallas_call(
        finish_kernel,
        in_specs=[SMEM] + [VMEM] * 9,
        out_specs=VMEM,
        out_shape=jax.ShapeDtypeStruct((HALF, WIDE), I16),
        scratch_shapes=[pltpu.VMEM((D, HALF), BF16), pltpu.VMEM((HALF, D), F32), pltpu.VMEM((HALF, D), F32)],
        compiler_params=params(24),
        cost_estimate=pl.CostEstimate(flops=5 * D**3, bytes_accessed=10 * D * D, transcendentals=0),
        name="finish",
    )(owners, high, low, qa, so_far, kept_g, rest, rest_beside, eig_in, eig_out)


def after(x, earlier):
    return lax.optimization_barrier((x, earlier))[0]


def local(grads, basis_slots, owners, eig_in, eig_out):
    def across(x):
        return lax.ppermute(x, "zh", CORE_SWAP)

    def beside(x):
        return lax.ppermute(x, "core", CORE_SWAP)

    def everywhere(x):
        x = x.reshape(64, 8, WIDE)
        return lax.all_to_all(x, ("dp", "zh"), split_axis=0, concat_axis=0, tiled=True).reshape(HALF, WIDE)

    slots = basis_slots[0, 0]
    send = pick(owners, slots, beside(give(owners, slots)))
    lead = across(send)
    other = beside(after(slots, send))
    send_rest, kept_a, kept_g = hold(owners, slots, other)
    rows = everywhere(after(quantize_rows(grads.reshape(HALF, D)), send_rest))
    rest = across(send_rest)
    high, low, qa, so_far = begin(
        owners, rows, beside(rows), kept_a, kept_g, lead, beside(lead), eig_in, eig_out
    )
    rest_beside = beside(after(rest, so_far))
    out = finish(owners, high, low, qa, so_far, kept_g, rest, rest_beside, eig_in, eig_out)
    return restore_rows(everywhere(out)).reshape(64, 1, 8, D)


def solution(mesh):
    fine = Mesh(mesh.devices.reshape(32, 2, 2), ("dp", "zh", "core"))
    grad = ("zh", "core")
    return jax.shard_map(
        local,
        mesh=fine,
        in_specs=(
            P(None, grad, "dp", None),
            P("dp", grad, None, None, None),
            P("dp", None),
            P("dp", None),
            P("dp", None),
        ),
        out_specs=P(None, grad, "dp", None),
        check_vma=False,
    )
```

time: 199 us -> 120 us (0.60)
  Pallas kernels: 104 us -> 26.1 us
  waiting for transfers between devices: 45.9 us -> 36.2 us
  starting transfers between devices: 15.1 us -> 20.4 us
  local copies, waits for them, and re-layouts: 3.94 us -> 6.53 us
    pallas_call x4 -> x5, Pallas kernels: 99.8 us -> 21.9 us  [the longest x1 9.93 us: begin(): pl.pallas_call(begin_kernel, in_specs=[SMEM] + [VMEM] * 8, out_specs=[VME...]
    ppermute x2, waiting for transfers between devices: 45.9 us -> 27.9 us  [across(): return lax.ppermute(x, 'zh', CORE_SWAP)]
    ppermute x4 -> x5, waiting for transfers between devices: 0.01 us -> 7.48 us  [beside(): return lax.ppermute(x, 'core', CORE_SWAP)]
    ppermute x2, starting transfers between devices: 3.6 us -> 7.27 us  [across(): return lax.ppermute(x, 'zh', CORE_SWAP)]
    unnamed x12 -> x20, local copies, waits for them, and re-layouts: 3.94 us -> 6.53 us
  transfers between devices with their start and end apart: 7 -> 8, of which waited for: 2 -> 6; matrix products, arithmetic and copies ran while one was open for 0% -> 0% of each run, Pallas kernels for 43% -> 11%
where the time goes in v2:
time: 120 us
  waiting for transfers between devices  36.2 us (30%)
  blocking collectives  30.7 us (26%)
  Pallas kernels  26.1 us (22%)
  starting transfers between devices  20.4 us (17%)
  local copies, waits for them, and re-layouts  6.53 us (5%)
    all_to_all x1, blocking collectives, everywhere(): lax.all_to_all(x, ('dp', 'zh'), split_axis=0, concat_axis=0, tiled=True)  30.7 us
    ppermute x2, waiting for transfers between devices, across(): return lax.ppermute(x, 'zh', CORE_SWAP)  27.9 us
    all_to_all x1, starting transfers between devices, everywhere(): lax.all_to_all(x, ('dp', 'zh'), split_axis=0, concat_axis=0, tiled=True)  12.7 us
    pallas_call x1, Pallas kernels, begin(): pl.pallas_call(begin_kernel, in_specs=[SMEM] + [VMEM] * 8, out_specs=[VME...  9.93 us
    ppermute x5, waiting for transfers between devices, beside(): return lax.ppermute(x, 'core', CORE_SWAP)  7.48 us
    ppermute x2, starting transfers between devices, across(): return lax.ppermute(x, 'zh', CORE_SWAP)  7.27 us
    pallas_call x1, Pallas kernels, finish(): pl.pallas_call(finish_kernel, in_specs=[SMEM] + [VMEM] * 9, out_specs=VME...  7.07 us
    unnamed x20, local copies, waits for them, and re-layouts  6.53 us
  transfers between devices with their start and end apart: 8, of which 6 were waited for; matrix products, arithmetic and copies ran while one was open for 0% of the time, Pallas kernels for 11%

profile of v2, /device:TPU:0, one launch (start us, length us, event | category | flops | bytes accessed | tf_op | source)
XLA Modules:
  0.0 120.1 jit_solution(11040335845348776944)
XLA Ops:
  0.0 0.0 copy-start.1
  0.0 0.7 copy-done.1
  0.7 1.6 %give.1 = bf16[1024,768]{1,0:T(8,128)(2,1)S(1)} custom-call(s32[2,2]{1,0:T(2,128)S(1)} %copy-done.1, bf16[2,1024,1024]{2,1,0:T(8,128)(2,1)} %bitcast.1.slots), custom_call_target="tpu_custom_call" | custom-call | bytes 3145728 | tf_op jit(solution)/shard_map/give/pallas_call | solution.py:130
  2.3 0.0 copy-start
  2.3 0.1 collective-permute-start
  2.4 3.4 %collective-permute-done.given = bf16[1024,768]{1,0:T(8,128)(2,1)S(1)} collective-permute-done((bf16[1024,768]{1,0:T(8,128)(2,1)S(1)}, bf16[1024,768]{1,0:T(8,128)(2,1)S(1)}, u32[]{:S(2)}, u32[]{:S(2)}) %collective-permute-start) | collective-permute-done | bytes 1572896 | tf_op jit(solution)/shard_map/ppermute | solution.py:304
  5.8 1.7 %pick.1 = bf16[1024,768]{1,0:T(8,128)(2,1)S(1)} custom-call(s32[2,2]{1,0:T(2,128)S(1)} %copy-done.1, bf16[2,1024,1024]{2,1,0:T(8,128)(2,1)} %bitcast.1.slots, bf16[1024,768]{1,0:T(8,128)(2,1)S(1)} %collective-permute-done.given), custom_call_target="tpu_custom_call" | custom-call | bytes 3145728 | tf_op jit(solution)/shard_map/pick/pallas_call | solution.py:156
  7.5 0.0 copy-start.2
  7.5 0.1 collective-permute-start.1
  7.6 4.4 %collective-permute-start.3 = (bf16[1024,768]{1,0:T(8,128)(2,1)S(1)}, bf16[1024,768]{1,0:T(8,128)(2,1)}, u32[]{:S(2)}, u32[]{:S(2)}) collective-permute-start(bf16[1024,768]{1,0:T(8,128)(2,1)S(1)} %pick.1), channel_id=1, source_target_pairs={{0,2},{2,0},{1,3},{3,1},{4,6},{6,4},{5,7},{7,5},{8,10},{10,8},{9,1... | collective-permute-start | bytes 4718600 | tf_op jit(solution)/shard_map/ppermute | solution.py:301
  12.0 0.0 copy-done
  12.0 2.1 %quantize.1 = s16[512,1152]{1,0:T(8,128)(2,1)} custom-call(f32[512,1024]{1,0:T(8,128)S(1)} %bitcast.10), custom_call_target="tpu_custom_call" | custom-call | bytes 3145728 | tf_op jit(solution)/shard_map/quantize/pallas_call | solution.py:70
  14.0 0.9 collective-permute-done.1.other
  14.9 0.0 copy-done.2
  14.9 1.7 %hold.1 = (bf16[1024,256]{1,0:T(8,128)(2,1)S(1)}, bf16[1024,1024]{1,0:T(8,128)(2,1)S(1)}, bf16[1024,1024]{1,0:T(8,128)(2,1)S(1)}) custom-call(s32[2,2]{1,0:T(2,128)S(1)} %copy-done.2, bf16[2,1024,1024]{2,1,0:T(8,128)(2,1)} %bitcast.1.slots, bf16[2,1024,1024]{2,1,0:T(8,128)(2,1)S(1)} %collective-permute-done.1.other), custom_call_target="tpu_custom_call" | custom-call | bytes 12582912 | tf_op jit(solution)/shard_map/hold/pallas_call | solution.py:180
  16.6 0.0 copy-start.3
  16.6 1.3 %copy-done.3 = bf16[1024,1024]{1,0:T(8,128)(2,1)} copy-done((bf16[1024,1024]{1,0:T(8,128)(2,1)}, bf16[1024,1024]{1,0:T(8,128)(2,1)S(1)}, u32[]{:S(2)}) %copy-start.3) | copy-done | bytes 2097176
  18.0 0.0 copy-start.6
  18.0 1.3 %copy-done.6 = bf16[1024,1024]{1,0:T(8,128)(2,1)} copy-done((bf16[1024,1024]{1,0:T(8,128)(2,1)}, bf16[1024,1024]{1,0:T(8,128)(2,1)S(1)}, u32[]{:S(2)}) %copy-start.6) | copy-done | bytes 2097176
  19.3 0.0 copy-start.8
  19.3 0.0 copy-start.9
  19.3 12.7 %all-to-all-start = ((s16[64,8,1152]{2,1,0:T(8,128)(2,1)}), s16[64,8,1152]{2,1,0:T(8,128)(2,1)S(1)}, u32[]{:S(2)}, u32[]{:S(2)}) async-start(s16[64,8,1152]{2,1,0:T(8,128)(2,1)} %bitcast.2), calls=%async_computation | async-start | bytes 2359296 | tf_op jit(solution)/shard_map/all_to_all | solution.py:308
  32.0 27.9 %collective-permute-done.3.lead = bf16[1024,768]{1,0:T(8,128)(2,1)} collective-permute-done((bf16[1024,768]{1,0:T(8,128)(2,1)S(1)}, bf16[1024,768]{1,0:T(8,128)(2,1)}, u32[]{:S(2)}, u32[]{:S(2)}) %collective-permute-start.3) | collective-permute-done | bytes 1572896 | tf_op jit(solution)/shard_map/ppermute | solution.py:301
  60.0 0.0 collective-permute-start.4
  60.0 0.8 all-to-all-done
  60.8 0.0 collective-permute-start.2
  60.8 2.9 %collective-permute-start.5 = (bf16[1024,256]{1,0:T(8,128)(2,1)S(1)}, bf16[1024,256]{1,0:T(8,128)(2,1)S(1)}, u32[]{:S(2)}, u32[]{:S(2)}) collective-permute-start(bf16[1024,256]{1,0:T(8,128)(2,1)S(1)} %get-tuple-element.16), channel_id=1, source_target_pairs={{0,2},{2,0},{1,3},{3,1},{4,6},{6,4},{5,7},{7,5},{8,10},{10,8},{9,1... | collective-permute-start | bytes 1572872 | tf_op jit(solution)/shard_map/ppermute | solution.py:301
  63.6 0.0 collective-permute-done.4.lead_beside
  63.6 1.4 %collective-permute-done.2.rows_beside = s16[512,1152]{1,0:T(8,128)(2,1)S(1)} collective-permute-done((s16[512,1152]{1,0:T(8,128)(2,1)S(1)}, s16[512,1152]{1,0:T(8,128)(2,1)S(1)}, u32[]{:S(2)}, u32[]{:S(2)}) %collective-permute-start.2) | collective-permute-done | bytes 1179680 | tf_op jit(solution)/shard_map/ppermute | solution.py:304
  65.1 0.0 copy-done.8
  65.1 0.0 copy-done.9
  65.1 0.0 copy-start.4
  65.1 1.6 %copy-done.4 = bf16[1024,1024]{1,0:T(8,128)(2,1)S(1)} copy-done((bf16[1024,1024]{1,0:T(8,128)(2,1)S(1)}, bf16[1024,1024]{1,0:T(8,128)(2,1)}, u32[]{:S(2)}) %copy-start.4) | copy-done | bytes 2097176
  66.7 0.0 copy-start.7
  66.7 1.6 %copy-done.7 = bf16[1024,1024]{1,0:T(8,128)(2,1)S(1)} copy-done((bf16[1024,1024]{1,0:T(8,128)(2,1)S(1)}, bf16[1024,1024]{1,0:T(8,128)(2,1)}, u32[]{:S(2)}) %copy-start.7) | copy-done | bytes 2097176
  68.3 0.0 copy-start.5
  68.3 9.9 %begin.1 = (bf16[1024,1024]{1,0:T(8,128)(2,1)S(1)}, bf16[1024,1024]{1,0:T(8,128)(2,1)S(1)}, bf16[1024,1024]{1,0:T(8,128)(2,1)S(1)}, f32[512,1024]{1,0:T(8,128)S(1)}) custom-call(s32[2,2]{1,0:T(2,128)S(1)} %copy-done.2, s16[512,1152]{1,0:T(8,128)(2,1)S(1)} %bitcast.12, s16[512,1152]{1,0:T(8,128)(2,1)S(1)} %collective-permute-done.2.rows_beside, ...), custom_call_target="tpu_custom_call" | custom-call | flops 7516192768 | bytes 20971520 | tf_op jit(solution)/shard_map/begin/pallas_call | solution.py:250
  78.2 0.0 collective-permute-done.5.rest
  78.2 0.2 collective-permute-start.6
  78.4 1.8 %collective-permute-done.6.rest_beside = bf16[1024,256]{1,0:T(8,128)(2,1)S(1)} collective-permute-done((bf16[1024,256]{1,0:T(8,128)(2,1)S(1)}, bf16[1024,256]{1,0:T(8,128)(2,1)S(1)}, u32[]{:S(2)}, u32[]{:S(2)}) %collective-permute-start.6) | collective-permute-done | bytes 524320 | tf_op jit(solution)/shard_map/ppermute | solution.py:304
  80.2 0.0 copy-done.5
  80.2 7.1 %finish.1 = s16[512,1152]{1,0:T(8,128)(2,1)S(1)} custom-call(s32[2,2]{1,0:T(2,128)S(1)} %copy-done.2, bf16[1024,1024]{1,0:T(8,128)(2,1)S(1)} %get-tuple-element.20.high_ref, bf16[1024,1024]{1,0:T(8,128)(2,1)S(1)} %get-tuple-element.21.low_ref, bf16[1024,1024]{1,0:T(8,128)(2,1)S(1)} %get-tuple-element.22.qa, f32[512,1024]{1,0:T(8,128)S(1)} %get-tuple-element.23.so_far, ...), custom_call_target="tpu_custom_call" | custom-call | flops 5368709120 | bytes 10485760 | tf_op jit(solution)/shard_map/finish/pallas_call | solution.py:283
  87.3 30.7 %all_to_all.10 = s16[64,8,1152]{2,1,0:T(8,128)(2,1)S(1)} all-to-all(s16[64,8,1152]{2,1,0:T(8,128)(2,1)S(1)} %bitcast.13), channel_id=1, replica_groups=mesh['dp'=32,'zh'=2,'core'=2] {'dp','zh'}, dimensions={0} | all-to-all | bytes 2359296 | tf_op jit(solution)/shard_map/all_to_all | solution.py:308
  117.9 2.1 %restore.1 = f32[512,1024]{1,0:T(8,128)} custom-call(s16[512,1152]{1,0:T(8,128)(2,1)S(1)} %bitcast.9), custom_call_target="tpu_custom_call" | custom-call | bytes 3145728 | tf_op jit(solution)/shard_map/restore/pallas_call | solution.py:88
Async XLA Ops:
  0.0 0.7 copy-start.1
  2.3 9.7 %copy-start = (f32[64,1,8,1024]{3,2,1,0:T(8,128)S(1)}, f32[64,1,8,1024]{3,2,1,0:T(8,128)}, u32[]{:S(2)}) copy-start(f32[64,1,8,1024]{3,2,1,0:T(8,128)} %param.5) | copy-start | bytes 6291460
  2.3 3.5 %collective-permute-start = (bf16[1024,768]{1,0:T(8,128)(2,1)S(1)}, bf16[1024,768]{1,0:T(8,128)(2,1)S(1)}, u32[]{:S(2)}, u32[]{:S(2)}) collective-permute-start(bf16[1024,768]{1,0:T(8,128)(2,1)S(1)} %give.1), channel_id=1, source_target_pairs={{0,1},{1,0},{2,3},{3,2},{4,5},{5,4},{6,7},{7,6},{8,9},{9,8},{10,11... | collective-permute-start | bytes 4718600 | tf_op jit(solution)/shard_map/ppermute | solution.py:304
  7.5 7.5 %copy-start.2 = (s32[2,2]{1,0:T(2,128)S(1)}, s32[2,2]{1,0:T(2,128)}, u32[]{:S(2)}) copy-start(s32[2,2]{1,0:T(2,128)} %owners.9) | copy-start | bytes 52
  7.5 7.4 %collective-permute-start.1 = (bf16[2,1024,1024]{2,1,0:T(8,128)(2,1)}, bf16[2,1024,1024]{2,1,0:T(8,128)(2,1)S(1)}, u32[]{:S(2)}, u32[]{:S(2)}) collective-permute-start(bf16[2,1024,1024]{2,1,0:T(8,128)(2,1)} %bitcast.1.slots), channel_id=1, source_target_pairs={{0,1},{1,0},{2,3},{3,2},{4,5},{5,4},{6,7},{7,6},{8,9},{9,8},{10,11... | collective-permute-start | bytes 12582920 | tf_op jit(solution)/shard_map/ppermute | solution.py:304
  7.6 52.4 %collective-permute-start.3 = (bf16[1024,768]{1,0:T(8,128)(2,1)S(1)}, bf16[1024,768]{1,0:T(8,128)(2,1)}, u32[]{:S(2)}, u32[]{:S(2)}) collective-permute-start(bf16[1024,768]{1,0:T(8,128)(2,1)S(1)} %pick.1), channel_id=1, source_target_pairs={{0,2},{2,0},{1,3},{3,1},{4,6},{6,4},{5,7},{7,5},{8,10},{10,8},{9,1... | collective-permute-start | bytes 4718600 | tf_op jit(solution)/shard_map/ppermute | solution.py:301
  16.6 1.3 %copy-start.3 = (bf16[1024,1024]{1,0:T(8,128)(2,1)}, bf16[1024,1024]{1,0:T(8,128)(2,1)S(1)}, u32[]{:S(2)}) copy-start(bf16[1024,1024]{1,0:T(8,128)(2,1)S(1)} %get-tuple-element.19.kept_g) | copy-start | bytes 6291460
  18.0 1.3 %copy-start.6 = (bf16[1024,1024]{1,0:T(8,128)(2,1)}, bf16[1024,1024]{1,0:T(8,128)(2,1)S(1)}, u32[]{:S(2)}) copy-start(bf16[1024,1024]{1,0:T(8,128)(2,1)S(1)} %get-tuple-element.18.kept_a) | copy-start | bytes 6291460
  19.3 45.8 %copy-start.8 = (f32[2,1024]{1,0:T(2,128)S(1)}, f32[2,1024]{1,0:T(2,128)}, u32[]{:S(2)}) copy-start(f32[2,1024]{1,0:T(2,128)} %eig_in.3) | copy-start | bytes 24580
  19.3 45.8 %copy-start.9 = (f32[2,1024]{1,0:T(2,128)S(1)}, f32[2,1024]{1,0:T(2,128)}, u32[]{:S(2)}) copy-start(f32[2,1024]{1,0:T(2,128)} %eig_out.3) | copy-start | bytes 24580
  19.3 41.5 %all-to-all-start = ((s16[64,8,1152]{2,1,0:T(8,128)(2,1)}), s16[64,8,1152]{2,1,0:T(8,128)(2,1)S(1)}, u32[]{:S(2)}, u32[]{:S(2)}) async-start(s16[64,8,1152]{2,1,0:T(8,128)(2,1)} %bitcast.2), calls=%async_computation | async-start | bytes 2359296 | tf_op jit(solution)/shard_map/all_to_all | solution.py:308
  60.0 3.7 %collective-permute-start.4 = (bf16[1024,768]{1,0:T(8,128)(2,1)}, bf16[1024,768]{1,0:T(8,128)(2,1)S(1)}, u32[]{:S(2)}, u32[]{:S(2)}) collective-permute-start(bf16[1024,768]{1,0:T(8,128)(2,1)} %collective-permute-done.3.lead), channel_id=1, source_target_pairs={{0,1},{1,0},{2,3},{3,2},{4,5},{5,4},{6,7},{7,6},{8,9},{9,8},{10,11... | collective-permute-start | bytes 4718600 | tf_op jit(solution)/shard_map/ppermute | solution.py:304
  60.8 4.3 %collective-permute-start.2 = (s16[512,1152]{1,0:T(8,128)(2,1)S(1)}, s16[512,1152]{1,0:T(8,128)(2,1)S(1)}, u32[]{:S(2)}, u32[]{:S(2)}) collective-permute-start(s16[512,1152]{1,0:T(8,128)(2,1)S(1)} %bitcast.11), channel_id=1, source_target_pairs={{0,1},{1,0},{2,3},{3,2},{4,5},{5,4},{6,7},{7,6},{8,9},{9,8},{10,11... | collective-permute-start | bytes 3538952 | tf_op jit(solution)/shard_map/ppermute | solution.py:304
  60.8 17.4 %collective-permute-start.5 = (bf16[1024,256]{1,0:T(8,128)(2,1)S(1)}, bf16[1024,256]{1,0:T(8,128)(2,1)S(1)}, u32[]{:S(2)}, u32[]{:S(2)}) collective-permute-start(bf16[1024,256]{1,0:T(8,128)(2,1)S(1)} %get-tuple-element.16), channel_id=1, source_target_pairs={{0,2},{2,0},{1,3},{3,1},{4,6},{6,4},{5,7},{7,5},{8,10},{10,8},{9,1... | collective-permute-start | bytes 1572872 | tf_op jit(solution)/shard_map/ppermute | solution.py:301
  65.1 1.6 %copy-start.4 = (bf16[1024,1024]{1,0:T(8,128)(2,1)S(1)}, bf16[1024,1024]{1,0:T(8,128)(2,1)}, u32[]{:S(2)}) copy-start(bf16[1024,1024]{1,0:T(8,128)(2,1)} %copy-done.3) | copy-start | bytes 6291460
  66.7 1.6 %copy-start.7 = (bf16[1024,1024]{1,0:T(8,128)(2,1)S(1)}, bf16[1024,1024]{1,0:T(8,128)(2,1)}, u32[]{:S(2)}) copy-start(bf16[1024,1024]{1,0:T(8,128)(2,1)} %copy-done.6) | copy-start | bytes 6291460
  68.3 11.9 %copy-start.5 = (bf16[1024,1024]{1,0:T(8,128)(2,1)S(1)}, bf16[1024,1024]{1,0:T(8,128)(2,1)}, u32[]{:S(2)}) copy-start(bf16[1024,1024]{1,0:T(8,128)(2,1)} %copy-done.3) | copy-start | bytes 6291460
  78.2 2.0 %collective-permute-start.6 = (bf16[1024,256]{1,0:T(8,128)(2,1)S(1)}, bf16[1024,256]{1,0:T(8,128)(2,1)S(1)}, u32[]{:S(2)}, u32[]{:S(2)}) collective-permute-start(bf16[1024,256]{1,0:T(8,128)(2,1)S(1)} %collective-permute-done.5.rest), channel_id=1, source_target_pairs={{0,1},{1,0},{2,3},{3,2},{4,5},{5,4},{6,7},{7,6},{8,9},{9,8},{10,11... | collective-permute-start | bytes 1572872 | tf_op jit(solution)/shard_map/ppermute | solution.py:304

commit v3 on v2

--- a/solution.py
+++ b/solution.py
@@ -165,26 +165,33 @@
     )(owners, slots, given)
 
 
-def hold_kernel(owners, slots, other, out, out_a, out_g, sem):
+def rest_kernel(owners, slots, other, out, sem):
     chip, core = lax.axis_index("zh"), lax.axis_index("core")
     has, beside, slot = place(owners, 1 - chip, 1, chip, core)
-    items = [(has, columns(slots.at[slot], HALF + core * QUARTER, QUARTER), out)]
-    items.append((beside, columns(other.at[slot], HALF + core * QUARTER, QUARTER), out))
+    items = []
+    for wanted, source in ((has, slots), (beside, other)):
+        items.append((wanted, columns(source.at[slot], HALF + core * QUARTER, QUARTER), out))
+    run_copies(items, sem)
+
+
+def keep_kernel(owners, slots, other, out_a, out_g, sem):
+    chip, core = lax.axis_index("zh"), lax.axis_index("core")
+    items = []
     for side, kept in enumerate((out_a, out_g)):
         has, beside, slot = place(owners, chip, side, chip, core)
         items += [(has, slots.at[slot], kept), (beside, other.at[slot], kept)]
     run_copies(items, sem)
 
 
-def hold(owners, slots, other):
-    return pl.pallas_call(
-        hold_kernel,
+def hold(kernel, shapes, owners, slots, other):
+    return pl.pallas_call(
+        kernel,
         in_specs=[SMEM, HBM, HBM],
-        out_specs=[VMEM] * 3,
-        out_shape=[jax.ShapeDtypeStruct((D, QUARTER), BF16)] + [jax.ShapeDtypeStruct((D, D), BF16)] * 2,
-        scratch_shapes=[pltpu.SemaphoreType.DMA((6,))],
+        out_specs=[VMEM] * len(shapes),
+        out_shape=[jax.ShapeDtypeStruct(shape, BF16) for shape in shapes],
+        scratch_shapes=[pltpu.SemaphoreType.DMA((4,))],
         compiler_params=params(10),
-        cost_estimate=pl.CostEstimate(flops=0, bytes_accessed=12 * D * D, transcendentals=0),
+        cost_estimate=pl.CostEstimate(flops=0, bytes_accessed=4 * D * D, transcendentals=0),
         name="hold",
     )(owners, slots, other)
 
@@ -311,12 +318,13 @@
     send = pick(owners, slots, beside(give(owners, slots)))
     lead = across(send)
     other = beside(after(slots, send))
-    send_rest, kept_a, kept_g = hold(owners, slots, other)
+    (send_rest,) = hold(rest_kernel, [(D, QUARTER)], owners, slots, other)
     rows = everywhere(after(quantize_rows(grads.reshape(HALF, D)), send_rest))
     rest = across(send_rest)
-    high, low, qa, so_far = begin(
-        owners, rows, beside(rows), kept_a, kept_g, lead, beside(lead), eig_in, eig_out
-    )
+    rows_beside = beside(rows)
+    kept_a, kept_g = hold(keep_kernel, [(D, D), (D, D)], owners, after(slots, rows), other)
+    lead_beside = beside(lead)
+    high, low, qa, so_far = begin(owners, rows, rows_beside, kept_a, kept_g, lead, lead_beside, eig_in, eig_out)
     rest_beside = beside(after(rest, so_far))
     out = finish(owners, high, low, qa, so_far, kept_g, rest, rest_beside, eig_in, eig_out)
     return restore_rows(everywhere(out)).reshape(64, 1, 8, D)

time: 120 us -> 118 us (0.983)
  local copies, waits for them, and re-layouts: 6.53 us -> 4.29 us
  waiting for transfers between devices: 36.2 us -> 38.3 us
  starting transfers between devices: 20.4 us -> 19.1 us
    ppermute x2, waiting for transfers between devices: 27.9 us -> 31.6 us  [across(): return lax.ppermute(x, 'zh', CORE_SWAP)]
    unnamed x20 -> x14, local copies, waits for them, and re-layouts: 6.53 us -> 4.29 us
    all_to_all x1, starting transfers between devices: 12.7 us -> 11.3 us  [everywhere(): lax.all_to_all(x, ('dp', 'zh'), split_axis=0, concat_axis=0, tiled=True)]
  transfers between devices with their start and end apart: 8 -> 8, of which waited for: 6 -> 5; matrix products, arithmetic and copies ran while one was open for 0% -> 0% of each run, Pallas kernels for 11% -> 11%
where the time goes in v3:
time: 118 us
  waiting for transfers between devices  38.3 us (32%)
  blocking collectives  29.9 us (25%)
  Pallas kernels  25.9 us (22%)
  starting transfers between devices  19.1 us (16%)
  local copies, waits for them, and re-layouts  4.29 us (4%)
    ppermute x2, waiting for transfers between devices, across(): return lax.ppermute(x, 'zh', CORE_SWAP)  31.6 us
    all_to_all x1, blocking collectives, everywhere(): lax.all_to_all(x, ('dp', 'zh'), split_axis=0, concat_axis=0, tiled=True)  29.9 us
    all_to_all x1, starting transfers between devices, everywhere(): lax.all_to_all(x, ('dp', 'zh'), split_axis=0, concat_axis=0, tiled=True)  11.3 us
    pallas_call x1, Pallas kernels, begin(): pl.pallas_call(begin_kernel, in_specs=[SMEM] + [VMEM] * 8, out_specs=[VME...  9.78 us
    ppermute x2, starting transfers between devices, across(): return lax.ppermute(x, 'zh', CORE_SWAP)  7.46 us
    pallas_call x1, Pallas kernels, finish(): pl.pallas_call(finish_kernel, in_specs=[SMEM] + [VMEM] * 9, out_specs=VME...  7.07 us
    ppermute x5, waiting for transfers between devices, beside(): return lax.ppermute(x, 'core', CORE_SWAP)  6.3 us
    unnamed x14, local copies, waits for them, and re-layouts  4.29 us
  transfers between devices with their start and end apart: 8, of which 5 were waited for; matrix products, arithmetic and copies ran while one was open for 0% of the time, Pallas kernels for 11%

profile of v3, /device:TPU:0, one launch (start us, length us, event | category | flops | bytes accessed | tf_op | source)
XLA Modules:
  0.0 117.7 jit_solution(10360580620693689463)
XLA Ops:
  0.0 0.0 copy-start.3
  0.0 0.7 copy-done.3
  0.7 1.8 %give.1 = bf16[1024,768]{1,0:T(8,128)(2,1)S(1)} custom-call(s32[2,2]{1,0:T(2,128)S(1)} %copy-done.3, bf16[2,1024,1024]{2,1,0:T(8,128)(2,1)} %bitcast.1.slots), custom_call_target="tpu_custom_call" | custom-call | bytes 3145728 | tf_op jit(solution)/shard_map/give/pallas_call | solution.py:130
  2.5 0.0 copy-start.2
  2.5 0.1 collective-permute-start
  2.6 3.4 %collective-permute-done.given = bf16[1024,768]{1,0:T(8,128)(2,1)S(1)} collective-permute-done((bf16[1024,768]{1,0:T(8,128)(2,1)S(1)}, bf16[1024,768]{1,0:T(8,128)(2,1)S(1)}, u32[]{:S(2)}, u32[]{:S(2)}) %collective-permute-start) | collective-permute-done | bytes 1572896 | tf_op jit(solution)/shard_map/ppermute | solution.py:311
  6.0 1.8 %pick.1 = bf16[1024,768]{1,0:T(8,128)(2,1)S(1)} custom-call(s32[2,2]{1,0:T(2,128)S(1)} %copy-done.3, bf16[2,1024,1024]{2,1,0:T(8,128)(2,1)} %bitcast.1.slots, bf16[1024,768]{1,0:T(8,128)(2,1)S(1)} %collective-permute-done.given), custom_call_target="tpu_custom_call" | custom-call | bytes 3145728 | tf_op jit(solution)/shard_map/pick/pallas_call | solution.py:156
  7.8 0.0 copy-start.4
  7.8 0.1 collective-permute-start.1
  7.9 4.3 %collective-permute-start.3 = (bf16[1024,768]{1,0:T(8,128)(2,1)S(1)}, bf16[1024,768]{1,0:T(8,128)(2,1)}, u32[]{:S(2)}, u32[]{:S(2)}) collective-permute-start(bf16[1024,768]{1,0:T(8,128)(2,1)S(1)} %pick.1), channel_id=1, source_target_pairs={{0,2},{2,0},{1,3},{3,1},{4,6},{6,4},{5,7},{7,5},{8,10},{10,8},{9,1... | collective-permute-start | bytes 4718600 | tf_op jit(solution)/shard_map/ppermute | solution.py:308
  12.2 0.0 copy-done.2
  12.2 2.0 %quantize.1 = s16[512,1152]{1,0:T(8,128)(2,1)} custom-call(f32[512,1024]{1,0:T(8,128)S(1)} %bitcast.10), custom_call_target="tpu_custom_call" | custom-call | bytes 3145728 | tf_op jit(solution)/shard_map/quantize/pallas_call | solution.py:70
  14.3 1.0 collective-permute-done.1.other
  15.3 0.0 copy-done.4
  15.3 0.0 copy-start
  15.3 0.6 hold.2
  15.9 1.3 %copy-done = bf16[2,1024,1024]{2,1,0:T(8,128)(2,1)} copy-done((bf16[2,1024,1024]{2,1,0:T(8,128)(2,1)}, bf16[2,1024,1024]{2,1,0:T(8,128)(2,1)S(1)}, u32[]{:S(2)}) %copy-start) | copy-done | bytes 4194328
  17.3 11.3 %all-to-all-start = ((s16[64,8,1152]{2,1,0:T(8,128)(2,1)}), s16[64,8,1152]{2,1,0:T(8,128)(2,1)S(1)}, u32[]{:S(2)}, u32[]{:S(2)}) async-start(s16[64,8,1152]{2,1,0:T(8,128)(2,1)} %bitcast.2), calls=%async_computation | async-start | bytes 2359296 | tf_op jit(solution)/shard_map/all_to_all | solution.py:315
  28.6 31.6 %collective-permute-done.3.lead = bf16[1024,768]{1,0:T(8,128)(2,1)} collective-permute-done((bf16[1024,768]{1,0:T(8,128)(2,1)S(1)}, bf16[1024,768]{1,0:T(8,128)(2,1)}, u32[]{:S(2)}, u32[]{:S(2)}) %collective-permute-start.3) | collective-permute-done | bytes 1572896 | tf_op jit(solution)/shard_map/ppermute | solution.py:308
  60.2 0.0 collective-permute-start.4
  60.2 0.4 all-to-all-done
  60.6 0.1 collective-permute-start.2
  60.7 3.2 %collective-permute-start.5 = (bf16[1024,256]{1,0:T(8,128)(2,1)S(1)}, bf16[1024,256]{1,0:T(8,128)(2,1)S(1)}, u32[]{:S(2)}, u32[]{:S(2)}) collective-permute-start(bf16[1024,256]{1,0:T(8,128)(2,1)S(1)} %hold.2), channel_id=1, source_target_pairs={{0,2},{2,0},{1,3},{3,1},{4,6},{6,4},{5,7},{7,5},{8,10},{10,8},{9,1... | collective-permute-start | bytes 1572872 | tf_op jit(solution)/shard_map/ppermute | solution.py:308
  63.9 0.0 copy-start.1
  63.9 2.2 %copy-done.1 = bf16[2,1024,1024]{2,1,0:T(8,128)(2,1)S(1)} copy-done((bf16[2,1024,1024]{2,1,0:T(8,128)(2,1)S(1)}, bf16[2,1024,1024]{2,1,0:T(8,128)(2,1)}, u32[]{:S(2)}) %copy-start.1) | copy-done | bytes 4194328
  66.1 0.0 copy-start.5
  66.1 0.0 copy-start.6
  66.1 0.6 hold.3
  66.7 0.0 collective-permute-done.4.lead_beside
  66.7 0.0 collective-permute-done.2.rows_beside
  66.7 0.0 copy-done.5
  66.8 0.0 copy-done.6
  66.8 9.8 %begin.1 = (bf16[1024,1024]{1,0:T(8,128)(2,1)S(1)}, bf16[1024,1024]{1,0:T(8,128)(2,1)S(1)}, bf16[1024,1024]{1,0:T(8,128)(2,1)S(1)}, f32[512,1024]{1,0:T(8,128)S(1)}) custom-call(s32[2,2]{1,0:T(2,128)S(1)} %copy-done.4, s16[512,1152]{1,0:T(8,128)(2,1)S(1)} %bitcast.12, s16[512,1152]{1,0:T(8,128)(2,1)S(1)} %collective-permute-done.2.rows_beside, ...), custom_call_target="tpu_custom_call" | custom-call | flops 7516192768 | bytes 20971520 | tf_op jit(solution)/shard_map/begin/pallas_call | solution.py:257
  76.6 0.0 collective-permute-done.5.rest
  76.6 0.1 collective-permute-start.6
  76.7 1.9 %collective-permute-done.6.rest_beside = bf16[1024,256]{1,0:T(8,128)(2,1)S(1)} collective-permute-done((bf16[1024,256]{1,0:T(8,128)(2,1)S(1)}, bf16[1024,256]{1,0:T(8,128)(2,1)S(1)}, u32[]{:S(2)}, u32[]{:S(2)}) %collective-permute-start.6) | collective-permute-done | bytes 524320 | tf_op jit(solution)/shard_map/ppermute | solution.py:311
  78.6 7.1 %finish.1 = s16[512,1152]{1,0:T(8,128)(2,1)S(1)} custom-call(s32[2,2]{1,0:T(2,128)S(1)} %copy-done.4, bf16[1024,1024]{1,0:T(8,128)(2,1)S(1)} %get-tuple-element.20.high_ref, bf16[1024,1024]{1,0:T(8,128)(2,1)S(1)} %get-tuple-element.21.low_ref, bf16[1024,1024]{1,0:T(8,128)(2,1)S(1)} %get-tuple-element.22.qa, f32[512,1024]{1,0:T(8,128)S(1)} %get-tuple-element.23.so_far, ...), custom_call_target="tpu_custom_call" | custom-call | flops 5368709120 | bytes 10485760 | tf_op jit(solution)/shard_map/finish/pallas_call | solution.py:290
  85.6 29.9 %all_to_all.10 = s16[64,8,1152]{2,1,0:T(8,128)(2,1)S(1)} all-to-all(s16[64,8,1152]{2,1,0:T(8,128)(2,1)S(1)} %bitcast.13), channel_id=1, replica_groups=mesh['dp'=32,'zh'=2,'core'=2] {'dp','zh'}, dimensions={0} | all-to-all | bytes 2359296 | tf_op jit(solution)/shard_map/all_to_all | solution.py:315
  115.6 2.1 %restore.1 = f32[512,1024]{1,0:T(8,128)} custom-call(s16[512,1152]{1,0:T(8,128)(2,1)S(1)} %bitcast.9), custom_call_target="tpu_custom_call" | custom-call | bytes 3145728 | tf_op jit(solution)/shard_map/restore/pallas_call | solution.py:88
Async XLA Ops:
  0.0 0.7 copy-start.3
  2.5 9.8 %copy-start.2 = (f32[64,1,8,1024]{3,2,1,0:T(8,128)S(1)}, f32[64,1,8,1024]{3,2,1,0:T(8,128)}, u32[]{:S(2)}) copy-start(f32[64,1,8,1024]{3,2,1,0:T(8,128)} %param.5) | copy-start | bytes 6291460
  2.5 3.5 %collective-permute-start = (bf16[1024,768]{1,0:T(8,128)(2,1)S(1)}, bf16[1024,768]{1,0:T(8,128)(2,1)S(1)}, u32[]{:S(2)}, u32[]{:S(2)}) collective-permute-start(bf16[1024,768]{1,0:T(8,128)(2,1)S(1)} %give.1), channel_id=1, source_target_pairs={{0,1},{1,0},{2,3},{3,2},{4,5},{5,4},{6,7},{7,6},{8,9},{9,8},{10,11... | collective-permute-start | bytes 4718600 | tf_op jit(solution)/shard_map/ppermute | solution.py:311
  7.8 7.5 %copy-start.4 = (s32[2,2]{1,0:T(2,128)S(1)}, s32[2,2]{1,0:T(2,128)}, u32[]{:S(2)}) copy-start(s32[2,2]{1,0:T(2,128)} %owners.11) | copy-start | bytes 52
  7.8 7.4 %collective-permute-start.1 = (bf16[2,1024,1024]{2,1,0:T(8,128)(2,1)}, bf16[2,1024,1024]{2,1,0:T(8,128)(2,1)S(1)}, u32[]{:S(2)}, u32[]{:S(2)}) collective-permute-start(bf16[2,1024,1024]{2,1,0:T(8,128)(2,1)} %bitcast.1.slots), channel_id=1, source_target_pairs={{0,1},{1,0},{2,3},{3,2},{4,5},{5,4},{6,7},{7,6},{8,9},{9,8},{10,11... | collective-permute-start | bytes 12582920 | tf_op jit(solution)/shard_map/ppermute | solution.py:311
  7.9 52.3 %collective-permute-start.3 = (bf16[1024,768]{1,0:T(8,128)(2,1)S(1)}, bf16[1024,768]{1,0:T(8,128)(2,1)}, u32[]{:S(2)}, u32[]{:S(2)}) collective-permute-start(bf16[1024,768]{1,0:T(8,128)(2,1)S(1)} %pick.1), channel_id=1, source_target_pairs={{0,2},{2,0},{1,3},{3,1},{4,6},{6,4},{5,7},{7,5},{8,10},{10,8},{9,1... | collective-permute-start | bytes 4718600 | tf_op jit(solution)/shard_map/ppermute | solution.py:308
  15.3 2.0 %copy-start = (bf16[2,1024,1024]{2,1,0:T(8,128)(2,1)}, bf16[2,1024,1024]{2,1,0:T(8,128)(2,1)S(1)}, u32[]{:S(2)}) copy-start(bf16[2,1024,1024]{2,1,0:T(8,128)(2,1)S(1)} %collective-permute-done.1.other) | copy-start | bytes 12582916
  17.3 43.4 %all-to-all-start = ((s16[64,8,1152]{2,1,0:T(8,128)(2,1)}), s16[64,8,1152]{2,1,0:T(8,128)(2,1)S(1)}, u32[]{:S(2)}, u32[]{:S(2)}) async-start(s16[64,8,1152]{2,1,0:T(8,128)(2,1)} %bitcast.2), calls=%async_computation | async-start | bytes 2359296 | tf_op jit(solution)/shard_map/all_to_all | solution.py:315
  60.2 6.5 %collective-permute-start.4 = (bf16[1024,768]{1,0:T(8,128)(2,1)}, bf16[1024,768]{1,0:T(8,128)(2,1)S(1)}, u32[]{:S(2)}, u32[]{:S(2)}) collective-permute-start(bf16[1024,768]{1,0:T(8,128)(2,1)} %collective-permute-done.3.lead), channel_id=1, source_target_pairs={{0,1},{1,0},{2,3},{3,2},{4,5},{5,4},{6,7},{7,6},{8,9},{9,8},{10,11... | collective-permute-start | bytes 4718600 | tf_op jit(solution)/shard_map/ppermute | solution.py:311
  60.6 6.1 %collective-permute-start.2 = (s16[512,1152]{1,0:T(8,128)(2,1)S(1)}, s16[512,1152]{1,0:T(8,128)(2,1)S(1)}, u32[]{:S(2)}, u32[]{:S(2)}) collective-permute-start(s16[512,1152]{1,0:T(8,128)(2,1)S(1)} %bitcast.11), channel_id=1, source_target_pairs={{0,1},{1,0},{2,3},{3,2},{4,5},{5,4},{6,7},{7,6},{8,9},{9,8},{10,11... | collective-permute-start | bytes 3538952 | tf_op jit(solution)/shard_map/ppermute | solution.py:311
  60.7 15.8 %collective-permute-start.5 = (bf16[1024,256]{1,0:T(8,128)(2,1)S(1)}, bf16[1024,256]{1,0:T(8,128)(2,1)S(1)}, u32[]{:S(2)}, u32[]{:S(2)}) collective-permute-start(bf16[1024,256]{1,0:T(8,128)(2,1)S(1)} %hold.2), channel_id=1, source_target_pairs={{0,2},{2,0},{1,3},{3,1},{4,6},{6,4},{5,7},{7,5},{8,10},{10,8},{9,1... | collective-permute-start | bytes 1572872 | tf_op jit(solution)/shard_map/ppermute | solution.py:308
  63.9 2.2 %copy-start.1 = (bf16[2,1024,1024]{2,1,0:T(8,128)(2,1)S(1)}, bf16[2,1024,1024]{2,1,0:T(8,128)(2,1)}, u32[]{:S(2)}) copy-start(bf16[2,1024,1024]{2,1,0:T(8,128)(2,1)} %copy-done) | copy-start | bytes 12582916
  66.1 0.7 copy-start.5
  66.1 0.7 copy-start.6
  76.6 2.0 %collective-permute-start.6 = (bf16[1024,256]{1,0:T(8,128)(2,1)S(1)}, bf16[1024,256]{1,0:T(8,128)(2,1)S(1)}, u32[]{:S(2)}, u32[]{:S(2)}) collective-permute-start(bf16[1024,256]{1,0:T(8,128)(2,1)S(1)} %collective-permute-done.5.rest), channel_id=1, source_target_pairs={{0,1},{1,0},{2,3},{3,2},{4,5},{5,4},{6,7},{7,6},{8,9},{9,8},{10,11... | collective-permute-start | bytes 1572872 | tf_op jit(solution)/shard_map/ppermute | solution.py:311

commit v4 on v3

--- a/solution.py
+++ b/solution.py
@@ -87,9 +87,9 @@
     rows = x.shape[0]
     return pl.pallas_call(
         restore_kernel,
-        grid=(4,),
-        in_specs=[pl.BlockSpec((rows // 4, WIDE), lambda i: (i, 0))],
-        out_specs=pl.BlockSpec((rows // 4, D), lambda i: (i, 0)),
+        grid=(2,),
+        in_specs=[pl.BlockSpec((rows // 2, WIDE), lambda i: (i, 0))],
+        out_specs=pl.BlockSpec((rows // 2, D), lambda i: (i, 0)),
         out_shape=jax.ShapeDtypeStruct((rows, D), F32),
         compiler_params=params(12),
         cost_estimate=pl.CostEstimate(flops=0, bytes_accessed=rows * D * 6, transcendentals=0),
@@ -230,11 +230,11 @@
     first = pl.multiple_of(core * 256, 256)
     eig_g = eig_out[pl.ds(chip, 1), which * HALF : (which + 1) * HALF]
     tops = jnp.concatenate([qg[pl.ds(first, 256), :], qg[pl.ds(first + HALF, 256), :]], axis=0)
-    for row in range(0, D, 512):
-        both = jnp.concatenate([high_ref[row : row + 512, :], low_ref[row : row + 512, :]], axis=0)
+    for row in range(0, D, 1024):
+        both = jnp.concatenate([high_ref[row : row + 1024, :], low_ref[row : row + 1024, :]], axis=0)
         eigen = jnp.dot(both, qg[...], preferred_element_type=F32)
-        eigen = eigen[:512] + eigen[512:]
-        eig_a = jnp.broadcast_to(eig_in[pl.ds(chip, 1), row : row + 512], (128, 512)).T[:, 0:1]
+        eigen = eigen[:1024] + eigen[1024:]
+        eig_a = jnp.broadcast_to(eig_in[pl.ds(chip, 1), row : row + 1024], (128, 1024)).T[:, 0:1]
         high, low = split(eigen / (eig_a * eig_g + 0.1))
         got = lax.dot_general(tops, high, (((1,), (1,)), ((), ())), preferred_element_type=F32)
         got = got + lax.dot_general(tops, low, (((1,), (1,)), ((), ())), preferred_element_type=F32)
@@ -248,7 +248,7 @@
     rotate(rows, rows_beside, qa, high_ref, low_ref)
 
     def add(row, col, got):
-        out_ref[:, col : col + 512] = got
+        out_ref[:, col : col + 1024] = got
 
     eigen_part(0, qg, high_ref, low_ref, eig_in, eig_out, add)
 
@@ -271,7 +271,7 @@
     gather(owners, 1, kept_g, HALF, rest, rest_beside, 0, QUARTER, qg)
 
     def add(row, col, got):
-        back[:, col : col + 512] = so_far[:, col : col + 512] + got
+        back[:, col : col + 1024] = so_far[:, col : col + 1024] + got
 
     eigen_part(1, qg, high_ref, low_ref, eig_in, eig_out, add)
     high, low = split(back[...])

time: 118 us -> 117 us (level)
  starting transfers between devices: 19.1 us -> 24.1 us
  Pallas kernels: 25.9 us -> 22.9 us
  waiting for transfers between devices: 38.3 us -> 36.2 us
    ppermute x5, starting transfers between devices: 0.36 us -> 3.52 us  [beside(): return lax.ppermute(x, 'core', CORE_SWAP)]
    all_to_all x1, starting transfers between devices: 11.3 us -> 12.8 us  [everywhere(): lax.all_to_all(x, ('dp', 'zh'), split_axis=0, concat_axis=0, tiled=True)]
    ppermute x5, waiting for transfers between devices: 6.3 us -> 4.98 us  [beside(): return lax.ppermute(x, 'core', CORE_SWAP)]
    pallas_call x1, Pallas kernels: 1.8 us -> 0.59 us  [give(): pl.pallas_call(give_kernel, in_specs=[SMEM, HBM], out_specs=VMEM, out_sha...]
where the time goes in v4:
time: 117 us
  waiting for transfers between devices  36.2 us (31%)
  blocking collectives  29.4 us (25%)
  starting transfers between devices  24.1 us (21%)
  Pallas kernels  22.9 us (20%)
  local copies, waits for them, and re-layouts  4.23 us (4%)
    ppermute x2, waiting for transfers between devices, across(): return lax.ppermute(x, 'zh', CORE_SWAP)  30.8 us
    all_to_all x1, blocking collectives, everywhere(): lax.all_to_all(x, ('dp', 'zh'), split_axis=0, concat_axis=0, tiled=True)  29.4 us
    all_to_all x1, starting transfers between devices, everywhere(): lax.all_to_all(x, ('dp', 'zh'), split_axis=0, concat_axis=0, tiled=True)  12.8 us
    pallas_call x1, Pallas kernels, begin(): pl.pallas_call(begin_kernel, in_specs=[SMEM] + [VMEM] * 8, out_specs=[VME...  9.75 us
    ppermute x2, starting transfers between devices, across(): return lax.ppermute(x, 'zh', CORE_SWAP)  7.78 us
    pallas_call x1, Pallas kernels, finish(): pl.pallas_call(finish_kernel, in_specs=[SMEM] + [VMEM] * 9, out_specs=VME...  6.93 us
    ppermute x5, waiting for transfers between devices, beside(): return lax.ppermute(x, 'core', CORE_SWAP)  4.98 us
    unnamed x14, local copies, waits for them, and re-layouts  4.23 us
  transfers between devices with their start and end apart: 8, of which 5 were waited for; matrix products, arithmetic and copies ran while one was open for 0% of the time, Pallas kernels for 11%

profile of v4, /device:TPU:0, one launch (start us, length us, event | category | flops | bytes accessed | tf_op | source)
XLA Modules:
  0.0 117.0 jit_solution(11767164493809715552)
XLA Ops:
  0.0 0.0 copy-start.3
  0.0 0.7 copy-done.3
  0.7 0.6 give.1
  1.3 0.0 copy-start.2
  1.3 0.4 collective-permute-start
  1.7 3.1 %collective-permute-done.given = bf16[1024,768]{1,0:T(8,128)(2,1)S(1)} collective-permute-done((bf16[1024,768]{1,0:T(8,128)(2,1)S(1)}, bf16[1024,768]{1,0:T(8,128)(2,1)S(1)}, u32[]{:S(2)}, u32[]{:S(2)}) %collective-permute-start) | collective-permute-done | bytes 1572896 | tf_op jit(solution)/shard_map/ppermute | solution.py:311
  4.8 0.7 pick.1
  5.5 0.0 copy-start.4
  5.5 1.5 %collective-permute-start.1 = (bf16[2,1024,1024]{2,1,0:T(8,128)(2,1)}, bf16[2,1024,1024]{2,1,0:T(8,128)(2,1)S(1)}, u32[]{:S(2)}, u32[]{:S(2)}) collective-permute-start(bf16[2,1024,1024]{2,1,0:T(8,128)(2,1)} %bitcast.1.slots), channel_id=1, source_target_pairs={{0,1},{1,0},{2,3},{3,2},{4,5},{5,4},{6,7},{7,6},{8,9},{9,8},{10,11... | collective-permute-start | bytes 12582920 | tf_op jit(solution)/shard_map/ppermute | solution.py:311
  7.0 4.6 %collective-permute-start.3 = (bf16[1024,768]{1,0:T(8,128)(2,1)S(1)}, bf16[1024,768]{1,0:T(8,128)(2,1)}, u32[]{:S(2)}, u32[]{:S(2)}) collective-permute-start(bf16[1024,768]{1,0:T(8,128)(2,1)S(1)} %pick.1), channel_id=1, source_target_pairs={{0,2},{2,0},{1,3},{3,1},{4,6},{6,4},{5,7},{7,5},{8,10},{10,8},{9,1... | collective-permute-start | bytes 4718600 | tf_op jit(solution)/shard_map/ppermute | solution.py:308
  11.6 0.0 copy-done.2
  11.6 2.0 %quantize.1 = s16[512,1152]{1,0:T(8,128)(2,1)} custom-call(f32[512,1024]{1,0:T(8,128)S(1)} %bitcast.10), custom_call_target="tpu_custom_call" | custom-call | bytes 3145728 | tf_op jit(solution)/shard_map/quantize/pallas_call | solution.py:70
  13.7 0.3 collective-permute-done.1.other
  14.0 0.0 copy-done.4
  14.0 0.0 copy-start
  14.0 0.6 hold.2
  14.6 1.3 %copy-done = bf16[2,1024,1024]{2,1,0:T(8,128)(2,1)} copy-done((bf16[2,1024,1024]{2,1,0:T(8,128)(2,1)}, bf16[2,1024,1024]{2,1,0:T(8,128)(2,1)S(1)}, u32[]{:S(2)}) %copy-start) | copy-done | bytes 4194328
  16.0 12.8 %all-to-all-start = ((s16[64,8,1152]{2,1,0:T(8,128)(2,1)}), s16[64,8,1152]{2,1,0:T(8,128)(2,1)S(1)}, u32[]{:S(2)}, u32[]{:S(2)}) async-start(s16[64,8,1152]{2,1,0:T(8,128)(2,1)} %bitcast.2), calls=%async_computation | async-start | bytes 2359296 | tf_op jit(solution)/shard_map/all_to_all | solution.py:315
  28.8 30.8 %collective-permute-done.3.lead = bf16[1024,768]{1,0:T(8,128)(2,1)} collective-permute-done((bf16[1024,768]{1,0:T(8,128)(2,1)S(1)}, bf16[1024,768]{1,0:T(8,128)(2,1)}, u32[]{:S(2)}, u32[]{:S(2)}) %collective-permute-start.3) | collective-permute-done | bytes 1572896 | tf_op jit(solution)/shard_map/ppermute | solution.py:308
  59.6 0.0 collective-permute-start.4
  59.6 0.4 all-to-all-done
  60.0 0.1 collective-permute-start.2
  60.1 3.2 %collective-permute-start.5 = (bf16[1024,256]{1,0:T(8,128)(2,1)S(1)}, bf16[1024,256]{1,0:T(8,128)(2,1)S(1)}, u32[]{:S(2)}, u32[]{:S(2)}) collective-permute-start(bf16[1024,256]{1,0:T(8,128)(2,1)S(1)} %hold.2), channel_id=1, source_target_pairs={{0,2},{2,0},{1,3},{3,1},{4,6},{6,4},{5,7},{7,5},{8,10},{10,8},{9,1... | collective-permute-start | bytes 1572872 | tf_op jit(solution)/shard_map/ppermute | solution.py:308
  63.3 0.0 copy-start.1
  63.3 2.2 %copy-done.1 = bf16[2,1024,1024]{2,1,0:T(8,128)(2,1)S(1)} copy-done((bf16[2,1024,1024]{2,1,0:T(8,128)(2,1)S(1)}, bf16[2,1024,1024]{2,1,0:T(8,128)(2,1)}, u32[]{:S(2)}) %copy-start.1) | copy-done | bytes 4194328
  65.5 0.0 copy-start.5
  65.5 0.0 copy-start.6
  65.5 0.8 hold.3
  66.2 0.0 collective-permute-done.4.lead_beside
  66.2 0.0 collective-permute-done.2.rows_beside
  66.3 0.0 copy-done.5
  66.3 0.0 copy-done.6
  66.3 9.8 %begin.1 = (bf16[1024,1024]{1,0:T(8,128)(2,1)S(1)}, bf16[1024,1024]{1,0:T(8,128)(2,1)S(1)}, bf16[1024,1024]{1,0:T(8,128)(2,1)S(1)}, f32[512,1024]{1,0:T(8,128)S(1)}) custom-call(s32[2,2]{1,0:T(2,128)S(1)} %copy-done.4, s16[512,1152]{1,0:T(8,128)(2,1)S(1)} %bitcast.12, s16[512,1152]{1,0:T(8,128)(2,1)S(1)} %collective-permute-done.2.rows_beside, ...), custom_call_target="tpu_custom_call" | custom-call | flops 7516192768 | bytes 20971520 | tf_op jit(solution)/shard_map/begin/pallas_call | solution.py:257
  76.0 0.0 collective-permute-done.5.rest
  76.0 1.5 %collective-permute-start.6 = (bf16[1024,256]{1,0:T(8,128)(2,1)S(1)}, bf16[1024,256]{1,0:T(8,128)(2,1)S(1)}, u32[]{:S(2)}, u32[]{:S(2)}) collective-permute-start(bf16[1024,256]{1,0:T(8,128)(2,1)S(1)} %collective-permute-done.5.rest), channel_id=1, source_target_pairs={{0,1},{1,0},{2,3},{3,2},{4,5},{5,4},{6,7},{7,6},{8,9},{9,8},{10,11... | collective-permute-start | bytes 1572872 | tf_op jit(solution)/shard_map/ppermute | solution.py:311
  77.5 1.5 %collective-permute-done.6.rest_beside = bf16[1024,256]{1,0:T(8,128)(2,1)S(1)} collective-permute-done((bf16[1024,256]{1,0:T(8,128)(2,1)S(1)}, bf16[1024,256]{1,0:T(8,128)(2,1)S(1)}, u32[]{:S(2)}, u32[]{:S(2)}) %collective-permute-start.6) | collective-permute-done | bytes 524320 | tf_op jit(solution)/shard_map/ppermute | solution.py:311
  79.1 6.9 %finish.1 = s16[512,1152]{1,0:T(8,128)(2,1)S(1)} custom-call(s32[2,2]{1,0:T(2,128)S(1)} %copy-done.4, bf16[1024,1024]{1,0:T(8,128)(2,1)S(1)} %get-tuple-element.20.high_ref, bf16[1024,1024]{1,0:T(8,128)(2,1)S(1)} %get-tuple-element.21.low_ref, bf16[1024,1024]{1,0:T(8,128)(2,1)S(1)} %get-tuple-element.22.qa, f32[512,1024]{1,0:T(8,128)S(1)} %get-tuple-element.23.so_far, ...), custom_call_target="tpu_custom_call" | custom-call | flops 5368709120 | bytes 10485760 | tf_op jit(solution)/shard_map/finish/pallas_call | solution.py:290
  86.0 29.4 %all_to_all.10 = s16[64,8,1152]{2,1,0:T(8,128)(2,1)S(1)} all-to-all(s16[64,8,1152]{2,1,0:T(8,128)(2,1)S(1)} %bitcast.13), channel_id=1, replica_groups=mesh['dp'=32,'zh'=2,'core'=2] {'dp','zh'}, dimensions={0} | all-to-all | bytes 2359296 | tf_op jit(solution)/shard_map/all_to_all | solution.py:315
  115.5 1.5 %restore.1 = f32[512,1024]{1,0:T(8,128)} custom-call(s16[512,1152]{1,0:T(8,128)(2,1)S(1)} %bitcast.9), custom_call_target="tpu_custom_call" | custom-call | bytes 3145728 | tf_op jit(solution)/shard_map/restore/pallas_call | solution.py:88
Async XLA Ops:
  0.0 0.7 copy-start.3
  1.3 10.3 %copy-start.2 = (f32[64,1,8,1024]{3,2,1,0:T(8,128)S(1)}, f32[64,1,8,1024]{3,2,1,0:T(8,128)}, u32[]{:S(2)}) copy-start(f32[64,1,8,1024]{3,2,1,0:T(8,128)} %param.5) | copy-start | bytes 6291460
  1.3 3.5 %collective-permute-start = (bf16[1024,768]{1,0:T(8,128)(2,1)S(1)}, bf16[1024,768]{1,0:T(8,128)(2,1)S(1)}, u32[]{:S(2)}, u32[]{:S(2)}) collective-permute-start(bf16[1024,768]{1,0:T(8,128)(2,1)S(1)} %give.1), channel_id=1, source_target_pairs={{0,1},{1,0},{2,3},{3,2},{4,5},{5,4},{6,7},{7,6},{8,9},{9,8},{10,11... | collective-permute-start | bytes 4718600 | tf_op jit(solution)/shard_map/ppermute | solution.py:311
  5.5 8.5 %copy-start.4 = (s32[2,2]{1,0:T(2,128)S(1)}, s32[2,2]{1,0:T(2,128)}, u32[]{:S(2)}) copy-start(s32[2,2]{1,0:T(2,128)} %owners.11) | copy-start | bytes 52
  5.5 8.5 %collective-permute-start.1 = (bf16[2,1024,1024]{2,1,0:T(8,128)(2,1)}, bf16[2,1024,1024]{2,1,0:T(8,128)(2,1)S(1)}, u32[]{:S(2)}, u32[]{:S(2)}) collective-permute-start(bf16[2,1024,1024]{2,1,0:T(8,128)(2,1)} %bitcast.1.slots), channel_id=1, source_target_pairs={{0,1},{1,0},{2,3},{3,2},{4,5},{5,4},{6,7},{7,6},{8,9},{9,8},{10,11... | collective-permute-start | bytes 12582920 | tf_op jit(solution)/shard_map/ppermute | solution.py:311
  7.0 52.6 %collective-permute-start.3 = (bf16[1024,768]{1,0:T(8,128)(2,1)S(1)}, bf16[1024,768]{1,0:T(8,128)(2,1)}, u32[]{:S(2)}, u32[]{:S(2)}) collective-permute-start(bf16[1024,768]{1,0:T(8,128)(2,1)S(1)} %pick.1), channel_id=1, source_target_pairs={{0,2},{2,0},{1,3},{3,1},{4,6},{6,4},{5,7},{7,5},{8,10},{10,8},{9,1... | collective-permute-start | bytes 4718600 | tf_op jit(solution)/shard_map/ppermute | solution.py:308
  14.0 2.0 %copy-start = (bf16[2,1024,1024]{2,1,0:T(8,128)(2,1)}, bf16[2,1024,1024]{2,1,0:T(8,128)(2,1)S(1)}, u32[]{:S(2)}) copy-start(bf16[2,1024,1024]{2,1,0:T(8,128)(2,1)S(1)} %collective-permute-done.1.other) | copy-start | bytes 12582916
  16.0 44.0 %all-to-all-start = ((s16[64,8,1152]{2,1,0:T(8,128)(2,1)}), s16[64,8,1152]{2,1,0:T(8,128)(2,1)S(1)}, u32[]{:S(2)}, u32[]{:S(2)}) async-start(s16[64,8,1152]{2,1,0:T(8,128)(2,1)} %bitcast.2), calls=%async_computation | async-start | bytes 2359296 | tf_op jit(solution)/shard_map/all_to_all | solution.py:315
  59.6 6.6 %collective-permute-start.4 = (bf16[1024,768]{1,0:T(8,128)(2,1)}, bf16[1024,768]{1,0:T(8,128)(2,1)S(1)}, u32[]{:S(2)}, u32[]{:S(2)}) collective-permute-start(bf16[1024,768]{1,0:T(8,128)(2,1)} %collective-permute-done.3.lead), channel_id=1, source_target_pairs={{0,1},{1,0},{2,3},{3,2},{4,5},{5,4},{6,7},{7,6},{8,9},{9,8},{10,11... | collective-permute-start | bytes 4718600 | tf_op jit(solution)/shard_map/ppermute | solution.py:311
  60.0 6.2 %collective-permute-start.2 = (s16[512,1152]{1,0:T(8,128)(2,1)S(1)}, s16[512,1152]{1,0:T(8,128)(2,1)S(1)}, u32[]{:S(2)}, u32[]{:S(2)}) collective-permute-start(s16[512,1152]{1,0:T(8,128)(2,1)S(1)} %bitcast.11), channel_id=1, source_target_pairs={{0,1},{1,0},{2,3},{3,2},{4,5},{5,4},{6,7},{7,6},{8,9},{9,8},{10,11... | collective-permute-start | bytes 3538952 | tf_op jit(solution)/shard_map/ppermute | solution.py:311
  60.1 15.9 %collective-permute-start.5 = (bf16[1024,256]{1,0:T(8,128)(2,1)S(1)}, bf16[1024,256]{1,0:T(8,128)(2,1)S(1)}, u32[]{:S(2)}, u32[]{:S(2)}) collective-permute-start(bf16[1024,256]{1,0:T(8,128)(2,1)S(1)} %hold.2), channel_id=1, source_target_pairs={{0,2},{2,0},{1,3},{3,1},{4,6},{6,4},{5,7},{7,5},{8,10},{10,8},{9,1... | collective-permute-start | bytes 1572872 | tf_op jit(solution)/shard_map/ppermute | solution.py:308
  63.3 2.2 %copy-start.1 = (bf16[2,1024,1024]{2,1,0:T(8,128)(2,1)S(1)}, bf16[2,1024,1024]{2,1,0:T(8,128)(2,1)}, u32[]{:S(2)}) copy-start(bf16[2,1024,1024]{2,1,0:T(8,128)(2,1)} %copy-done) | copy-start | bytes 12582916
  65.5 0.8 copy-start.5
  65.5 0.8 copy-start.6
  76.0 3.0 %collective-permute-start.6 = (bf16[1024,256]{1,0:T(8,128)(2,1)S(1)}, bf16[1024,256]{1,0:T(8,128)(2,1)S(1)}, u32[]{:S(2)}, u32[]{:S(2)}) collective-permute-start(bf16[1024,256]{1,0:T(8,128)(2,1)S(1)} %collective-permute-done.5.rest), channel_id=1, source_target_pairs={{0,1},{1,0},{2,3},{3,2},{4,5},{5,4},{6,7},{7,6},{8,9},{9,8},{10,11... | collective-permute-start | bytes 1572872 | tf_op jit(solution)/shard_map/ppermute | solution.py:311

commit v5 on v4

--- a/solution.py
+++ b/solution.py
@@ -190,7 +190,7 @@
         out_specs=[VMEM] * len(shapes),
         out_shape=[jax.ShapeDtypeStruct(shape, BF16) for shape in shapes],
         scratch_shapes=[pltpu.SemaphoreType.DMA((4,))],
-        compiler_params=params(10),
+        compiler_params=params(48),
         cost_estimate=pl.CostEstimate(flops=0, bytes_accessed=4 * D * D, transcendentals=0),
         name="hold",
     )(owners, slots, other)

time: 117 us -> 118 us (level)
  starting transfers between devices: 24.1 us -> 18.7 us
  Pallas kernels: 22.9 us -> 27.2 us
  waiting for transfers between devices: 36.2 us -> 38.4 us
  local copies, waits for them, and re-layouts: 4.23 us -> 2.67 us
    ppermute x5, starting transfers between devices: 3.52 us -> 0.18 us  [beside(): return lax.ppermute(x, 'core', CORE_SWAP)]
    pallas_call x2, Pallas kernels: 1.36 us -> 3.83 us  [hold(): pl.pallas_call(kernel, in_specs=[SMEM, HBM, HBM], out_specs=[VMEM] * len(...]
    unnamed x14 -> x12, local copies, waits for them, and re-layouts: 4.23 us -> 2.67 us
    all_to_all x1, starting transfers between devices: 12.8 us -> 11.5 us  [everywhere(): lax.all_to_all(x, ('dp', 'zh'), split_axis=0, concat_axis=0, tiled=True)]
    ppermute x5, waiting for transfers between devices: 4.98 us -> 6.23 us  [beside(): return lax.ppermute(x, 'core', CORE_SWAP)]
  transfers between devices with their start and end apart: 8 -> 8, of which waited for: 5 -> 6; matrix products, arithmetic and copies ran while one was open for 0% -> 0% of each run, Pallas kernels for 11% -> 13%
where the time goes in v5:
time: 118 us; the launch traced here: 117 us
  waiting for transfers between devices  38.4 us (33%)
  blocking collectives  29.7 us (25%)
  Pallas kernels  27.2 us (23%)
  starting transfers between devices  18.7 us (16%)
  local copies, waits for them, and re-layouts  2.67 us (2%)
    ppermute x2, waiting for transfers between devices, across(): return lax.ppermute(x, 'zh', CORE_SWAP)  31.2 us
    all_to_all x1, blocking collectives, everywhere(): lax.all_to_all(x, ('dp', 'zh'), split_axis=0, concat_axis=0, tiled=True)  29.7 us
    all_to_all x1, starting transfers between devices, everywhere(): lax.all_to_all(x, ('dp', 'zh'), split_axis=0, concat_axis=0, tiled=True)  11.5 us
    pallas_call x1, Pallas kernels, begin(): pl.pallas_call(begin_kernel, in_specs=[SMEM] + [VMEM] * 8, out_specs=[VME...  9.62 us
    ppermute x2, starting transfers between devices, across(): return lax.ppermute(x, 'zh', CORE_SWAP)  7.05 us
    pallas_call x1, Pallas kernels, finish(): pl.pallas_call(finish_kernel, in_specs=[SMEM] + [VMEM] * 9, out_specs=VME...  6.85 us
    ppermute x5, waiting for transfers between devices, beside(): return lax.ppermute(x, 'core', CORE_SWAP)  6.23 us
    pallas_call x2, Pallas kernels, hold(): pl.pallas_call(kernel, in_specs=[SMEM, HBM, HBM], out_specs=[VMEM] * len(...  3.83 us
  transfers between devices with their start and end apart: 8, of which 6 were waited for; matrix products, arithmetic and copies ran while one was open for 0% of the time, Pallas kernels for 13%

profile of v5, /device:TPU:0, one launch (start us, length us, event | category | flops | bytes accessed | tf_op | source)
XLA Modules:
  0.0 116.9 jit_solution(4303481872171981549)
XLA Ops:
  0.0 0.0 copy-start.1
  0.0 0.7 copy-done.1
  0.7 1.6 %give.1 = bf16[1024,768]{1,0:T(8,128)(2,1)S(1)} custom-call(s32[2,2]{1,0:T(2,128)S(1)} %copy-done.1, bf16[2,1024,1024]{2,1,0:T(8,128)(2,1)} %bitcast.1.slots), custom_call_target="tpu_custom_call" | custom-call | bytes 3145728 | tf_op jit(solution)/shard_map/give/pallas_call | solution.py:130
  2.3 0.0 copy-start
  2.3 0.1 collective-permute-start
  2.4 3.4 %collective-permute-done.given = bf16[1024,768]{1,0:T(8,128)(2,1)S(1)} collective-permute-done((bf16[1024,768]{1,0:T(8,128)(2,1)S(1)}, bf16[1024,768]{1,0:T(8,128)(2,1)S(1)}, u32[]{:S(2)}, u32[]{:S(2)}) %collective-permute-start) | collective-permute-done | bytes 1572896 | tf_op jit(solution)/shard_map/ppermute | solution.py:311
  5.8 1.7 %pick.1 = bf16[1024,768]{1,0:T(8,128)(2,1)S(1)} custom-call(s32[2,2]{1,0:T(2,128)S(1)} %copy-done.1, bf16[2,1024,1024]{2,1,0:T(8,128)(2,1)} %bitcast.1.slots, bf16[1024,768]{1,0:T(8,128)(2,1)S(1)} %collective-permute-done.given), custom_call_target="tpu_custom_call" | custom-call | bytes 3145728 | tf_op jit(solution)/shard_map/pick/pallas_call | solution.py:156
  7.5 0.0 copy-start.2
  7.5 0.1 collective-permute-start.1
  7.6 4.4 %collective-permute-start.3 = (bf16[1024,768]{1,0:T(8,128)(2,1)S(1)}, bf16[1024,768]{1,0:T(8,128)(2,1)}, u32[]{:S(2)}, u32[]{:S(2)}) collective-permute-start(bf16[1024,768]{1,0:T(8,128)(2,1)S(1)} %pick.1), channel_id=1, source_target_pairs={{0,2},{2,0},{1,3},{3,1},{4,6},{6,4},{5,7},{7,5},{8,10},{10,8},{9,1... | collective-permute-start | bytes 4718600 | tf_op jit(solution)/shard_map/ppermute | solution.py:308
  12.0 0.0 copy-done
  12.0 2.0 %quantize.1 = s16[512,1152]{1,0:T(8,128)(2,1)} custom-call(f32[512,1024]{1,0:T(8,128)S(1)} %bitcast.10), custom_call_target="tpu_custom_call" | custom-call | bytes 3145728 | tf_op jit(solution)/shard_map/quantize/pallas_call | solution.py:70
  14.0 0.9 collective-permute-done.1.other
  14.9 0.0 copy-start.5
  14.9 2.0 %copy-done.5 = bf16[2,1024,1024]{2,1,0:T(8,128)(2,1)} copy-done((bf16[2,1024,1024]{2,1,0:T(8,128)(2,1)}, bf16[2,1024,1024]{2,1,0:T(8,128)(2,1)S(1)}, u32[]{:S(2)}) %copy-start.5) | copy-done | bytes 4194328
  16.9 0.0 copy-done.2
  16.9 1.6 %hold.2 = bf16[1024,256]{1,0:T(8,128)(2,1)S(1)} custom-call(s32[2,2]{1,0:T(2,128)S(1)} %copy-done.2, bf16[2,1024,1024]{2,1,0:T(8,128)(2,1)} %bitcast.1.slots, bf16[2,1024,1024]{2,1,0:T(8,128)(2,1)} %copy-done.5), custom_call_target="tpu_custom_call" | custom-call | bytes 4194304 | tf_op jit(solution)/shard_map/hold/pallas_call | solution.py:187
  18.6 11.5 %all-to-all-start = ((s16[64,8,1152]{2,1,0:T(8,128)(2,1)}), s16[64,8,1152]{2,1,0:T(8,128)(2,1)S(1)}, u32[]{:S(2)}, u32[]{:S(2)}) async-start(s16[64,8,1152]{2,1,0:T(8,128)(2,1)} %bitcast.2), calls=%async_computation | async-start | bytes 2359296 | tf_op jit(solution)/shard_map/all_to_all | solution.py:315
  30.1 29.9 %collective-permute-done.3.lead = bf16[1024,768]{1,0:T(8,128)(2,1)} collective-permute-done((bf16[1024,768]{1,0:T(8,128)(2,1)S(1)}, bf16[1024,768]{1,0:T(8,128)(2,1)}, u32[]{:S(2)}, u32[]{:S(2)}) %collective-permute-start.3) | collective-permute-done | bytes 1572896 | tf_op jit(solution)/shard_map/ppermute | solution.py:308
  60.0 0.0 collective-permute-start.4
  60.0 0.9 all-to-all-done
  61.0 0.0 copy-start.3
  61.0 0.0 copy-start.4
  61.0 0.0 collective-permute-start.2
  61.0 2.7 %collective-permute-start.5 = (bf16[1024,256]{1,0:T(8,128)(2,1)S(1)}, bf16[1024,256]{1,0:T(8,128)(2,1)S(1)}, u32[]{:S(2)}, u32[]{:S(2)}) collective-permute-start(bf16[1024,256]{1,0:T(8,128)(2,1)S(1)} %hold.2), channel_id=1, source_target_pairs={{0,2},{2,0},{1,3},{3,1},{4,6},{6,4},{5,7},{7,5},{8,10},{10,8},{9,1... | collective-permute-start | bytes 1572872 | tf_op jit(solution)/shard_map/ppermute | solution.py:308
  63.6 2.2 %hold.3 = (bf16[1024,1024]{1,0:T(8,128)(2,1)S(1)}, bf16[1024,1024]{1,0:T(8,128)(2,1)S(1)}) custom-call(s32[2,2]{1,0:T(2,128)S(1)} %copy-done.2, bf16[2,1024,1024]{2,1,0:T(8,128)(2,1)} %bitcast.1.slots, bf16[2,1024,1024]{2,1,0:T(8,128)(2,1)} %copy-done.5), custom_call_target="tpu_custom_call" | custom-call | bytes 4194304 | tf_op jit(solution)/shard_map/hold/pallas_call | solution.py:187
  65.8 0.0 collective-permute-done.4.lead_beside
  65.8 0.0 collective-permute-done.2.rows_beside
  65.8 0.0 copy-done.3
  65.9 0.0 copy-done.4
  65.9 9.6 %begin.1 = (bf16[1024,1024]{1,0:T(8,128)(2,1)S(1)}, bf16[1024,1024]{1,0:T(8,128)(2,1)S(1)}, bf16[1024,1024]{1,0:T(8,128)(2,1)S(1)}, f32[512,1024]{1,0:T(8,128)S(1)}) custom-call(s32[2,2]{1,0:T(2,128)S(1)} %copy-done.2, s16[512,1152]{1,0:T(8,128)(2,1)S(1)} %bitcast.12, s16[512,1152]{1,0:T(8,128)(2,1)S(1)} %collective-permute-done.2.rows_beside, ...), custom_call_target="tpu_custom_call" | custom-call | flops 7516192768 | bytes 20971520 | tf_op jit(solution)/shard_map/begin/pallas_call | solution.py:257
  75.5 1.3 %collective-permute-done.5.rest = bf16[1024,256]{1,0:T(8,128)(2,1)S(1)} collective-permute-done((bf16[1024,256]{1,0:T(8,128)(2,1)S(1)}, bf16[1024,256]{1,0:T(8,128)(2,1)S(1)}, u32[]{:S(2)}, u32[]{:S(2)}) %collective-permute-start.5) | collective-permute-done | bytes 524320 | tf_op jit(solution)/shard_map/ppermute | solution.py:308
  76.8 0.0 collective-permute-start.6
  76.8 1.9 %collective-permute-done.6.rest_beside = bf16[1024,256]{1,0:T(8,128)(2,1)S(1)} collective-permute-done((bf16[1024,256]{1,0:T(8,128)(2,1)S(1)}, bf16[1024,256]{1,0:T(8,128)(2,1)S(1)}, u32[]{:S(2)}, u32[]{:S(2)}) %collective-permute-start.6) | collective-permute-done | bytes 524320 | tf_op jit(solution)/shard_map/ppermute | solution.py:311
  78.7 6.9 %finish.1 = s16[512,1152]{1,0:T(8,128)(2,1)S(1)} custom-call(s32[2,2]{1,0:T(2,128)S(1)} %copy-done.2, bf16[1024,1024]{1,0:T(8,128)(2,1)S(1)} %get-tuple-element.20.high_ref, bf16[1024,1024]{1,0:T(8,128)(2,1)S(1)} %get-tuple-element.21.low_ref, bf16[1024,1024]{1,0:T(8,128)(2,1)S(1)} %get-tuple-element.22.qa, f32[512,1024]{1,0:T(8,128)S(1)} %get-tuple-element.23.so_far, ...), custom_call_target="tpu_custom_call" | custom-call | flops 5368709120 | bytes 10485760 | tf_op jit(solution)/shard_map/finish/pallas_call | solution.py:290
  85.6 29.7 %all_to_all.10 = s16[64,8,1152]{2,1,0:T(8,128)(2,1)S(1)} all-to-all(s16[64,8,1152]{2,1,0:T(8,128)(2,1)S(1)} %bitcast.13), channel_id=1, replica_groups=mesh['dp'=32,'zh'=2,'core'=2] {'dp','zh'}, dimensions={0} | all-to-all | bytes 2359296 | tf_op jit(solution)/shard_map/all_to_all | solution.py:315
  115.3 1.5 %restore.1 = f32[512,1024]{1,0:T(8,128)} custom-call(s16[512,1152]{1,0:T(8,128)(2,1)S(1)} %bitcast.9), custom_call_target="tpu_custom_call" | custom-call | bytes 3145728 | tf_op jit(solution)/shard_map/restore/pallas_call | solution.py:88
Async XLA Ops:
  0.0 0.7 copy-start.1
  2.3 9.7 %copy-start = (f32[64,1,8,1024]{3,2,1,0:T(8,128)S(1)}, f32[64,1,8,1024]{3,2,1,0:T(8,128)}, u32[]{:S(2)}) copy-start(f32[64,1,8,1024]{3,2,1,0:T(8,128)} %param.5) | copy-start | bytes 6291460
  2.3 3.5 %collective-permute-start = (bf16[1024,768]{1,0:T(8,128)(2,1)S(1)}, bf16[1024,768]{1,0:T(8,128)(2,1)S(1)}, u32[]{:S(2)}, u32[]{:S(2)}) collective-permute-start(bf16[1024,768]{1,0:T(8,128)(2,1)S(1)} %give.1), channel_id=1, source_target_pairs={{0,1},{1,0},{2,3},{3,2},{4,5},{5,4},{6,7},{7,6},{8,9},{9,8},{10,11... | collective-permute-start | bytes 4718600 | tf_op jit(solution)/shard_map/ppermute | solution.py:311
  7.5 9.4 %copy-start.2 = (s32[2,2]{1,0:T(2,128)S(1)}, s32[2,2]{1,0:T(2,128)}, u32[]{:S(2)}) copy-start(s32[2,2]{1,0:T(2,128)} %owners.11) | copy-start | bytes 52
  7.5 7.4 %collective-permute-start.1 = (bf16[2,1024,1024]{2,1,0:T(8,128)(2,1)}, bf16[2,1024,1024]{2,1,0:T(8,128)(2,1)S(1)}, u32[]{:S(2)}, u32[]{:S(2)}) collective-permute-start(bf16[2,1024,1024]{2,1,0:T(8,128)(2,1)} %bitcast.1.slots), channel_id=1, source_target_pairs={{0,1},{1,0},{2,3},{3,2},{4,5},{5,4},{6,7},{7,6},{8,9},{9,8},{10,11... | collective-permute-start | bytes 12582920 | tf_op jit(solution)/shard_map/ppermute | solution.py:311
  7.6 52.4 %collective-permute-start.3 = (bf16[1024,768]{1,0:T(8,128)(2,1)S(1)}, bf16[1024,768]{1,0:T(8,128)(2,1)}, u32[]{:S(2)}, u32[]{:S(2)}) collective-permute-start(bf16[1024,768]{1,0:T(8,128)(2,1)S(1)} %pick.1), channel_id=1, source_target_pairs={{0,2},{2,0},{1,3},{3,1},{4,6},{6,4},{5,7},{7,5},{8,10},{10,8},{9,1... | collective-permute-start | bytes 4718600 | tf_op jit(solution)/shard_map/ppermute | solution.py:308
  14.9 2.0 %copy-start.5 = (bf16[2,1024,1024]{2,1,0:T(8,128)(2,1)}, bf16[2,1024,1024]{2,1,0:T(8,128)(2,1)S(1)}, u32[]{:S(2)}) copy-start(bf16[2,1024,1024]{2,1,0:T(8,128)(2,1)S(1)} %collective-permute-done.1.other) | copy-start | bytes 12582916
  18.6 42.4 %all-to-all-start = ((s16[64,8,1152]{2,1,0:T(8,128)(2,1)}), s16[64,8,1152]{2,1,0:T(8,128)(2,1)S(1)}, u32[]{:S(2)}, u32[]{:S(2)}) async-start(s16[64,8,1152]{2,1,0:T(8,128)(2,1)} %bitcast.2), calls=%async_computation | async-start | bytes 2359296 | tf_op jit(solution)/shard_map/all_to_all | solution.py:315
  60.0 5.8 %collective-permute-start.4 = (bf16[1024,768]{1,0:T(8,128)(2,1)}, bf16[1024,768]{1,0:T(8,128)(2,1)S(1)}, u32[]{:S(2)}, u32[]{:S(2)}) collective-permute-start(bf16[1024,768]{1,0:T(8,128)(2,1)} %collective-permute-done.3.lead), channel_id=1, source_target_pairs={{0,1},{1,0},{2,3},{3,2},{4,5},{5,4},{6,7},{7,6},{8,9},{9,8},{10,11... | collective-permute-start | bytes 4718600 | tf_op jit(solution)/shard_map/ppermute | solution.py:311
  61.0 4.9 %copy-start.3 = (f32[2,1024]{1,0:T(2,128)S(1)}, f32[2,1024]{1,0:T(2,128)}, u32[]{:S(2)}) copy-start(f32[2,1024]{1,0:T(2,128)} %eig_in.3) | copy-start | bytes 24580
  61.0 4.9 %copy-start.4 = (f32[2,1024]{1,0:T(2,128)S(1)}, f32[2,1024]{1,0:T(2,128)}, u32[]{:S(2)}) copy-start(f32[2,1024]{1,0:T(2,128)} %eig_out.3) | copy-start | bytes 24580
  61.0 4.9 %collective-permute-start.2 = (s16[512,1152]{1,0:T(8,128)(2,1)S(1)}, s16[512,1152]{1,0:T(8,128)(2,1)S(1)}, u32[]{:S(2)}, u32[]{:S(2)}) collective-permute-start(s16[512,1152]{1,0:T(8,128)(2,1)S(1)} %bitcast.11), channel_id=1, source_target_pairs={{0,1},{1,0},{2,3},{3,2},{4,5},{5,4},{6,7},{7,6},{8,9},{9,8},{10,11... | collective-permute-start | bytes 3538952 | tf_op jit(solution)/shard_map/ppermute | solution.py:311
  61.0 15.9 %collective-permute-start.5 = (bf16[1024,256]{1,0:T(8,128)(2,1)S(1)}, bf16[1024,256]{1,0:T(8,128)(2,1)S(1)}, u32[]{:S(2)}, u32[]{:S(2)}) collective-permute-start(bf16[1024,256]{1,0:T(8,128)(2,1)S(1)} %hold.2), channel_id=1, source_target_pairs={{0,2},{2,0},{1,3},{3,1},{4,6},{6,4},{5,7},{7,5},{8,10},{10,8},{9,1... | collective-permute-start | bytes 1572872 | tf_op jit(solution)/shard_map/ppermute | solution.py:308
  76.8 1.9 %collective-permute-start.6 = (bf16[1024,256]{1,0:T(8,128)(2,1)S(1)}, bf16[1024,256]{1,0:T(8,128)(2,1)S(1)}, u32[]{:S(2)}, u32[]{:S(2)}) collective-permute-start(bf16[1024,256]{1,0:T(8,128)(2,1)S(1)} %collective-permute-done.5.rest), channel_id=1, source_target_pairs={{0,1},{1,0},{2,3},{3,2},{4,5},{5,4},{6,7},{7,6},{8,9},{9,8},{10,11... | collective-permute-start | bytes 1572872 | tf_op jit(solution)/shard_map/ppermute | solution.py:311
